TPU v7x, 128 devices: a whole 4x4x4 slice. The times are simulated.
128 devices in a mesh: section: 2 (over z_lo), ctx: 32 (over y, x, core), wsh: 2 (over z_hi).
Axes of the slice: x: 4, y: 4, z: 4 (z_hi: 2, z_lo: 2; z = z_hi * 2 + z_lo), core: 2. Of those that a mesh axis runs over, the one named last changes fastest.
Arguments:
- inputs: bfloat16 [2, 2, 4096, 576], P(None, 'wsh', 'ctx'), may hold values from -6 to 6
- cotangent: bfloat16 [2, 2, 4096, 576], P(None, 'wsh', 'ctx'), may hold values from -6 to 6
- positions: int32 [2, 2, 4096], P(None, 'wsh', 'ctx'), may hold values from 0 to 4095, as said below
- norm_attn: bfloat16 [2, 576], P('section', 'wsh'), may hold values from 0.5 to 1.5
- w_query: bfloat16 [2, 576, 576], P('section', 'wsh'), may hold values from -0.25 to 0.25
- w_key: bfloat16 [2, 576, 192], P('section', 'wsh'), may hold values from -0.25 to 0.25
- w_value: bfloat16 [2, 576, 192], P('section', 'wsh'), may hold values from -0.25 to 0.25
- w_out: bfloat16 [2, 576, 576], P('section', 'wsh'), may hold values from -2 to 2
- norm_mlp: bfloat16 [2, 576], P('section', 'wsh'), may hold values from 0.5 to 1.5
- w_gate: bfloat16 [2, 576, 1536], P('section', 'wsh'), may hold values from -0.25 to 0.25
- w_up: bfloat16 [2, 576, 1536], P('section', 'wsh'), may hold values from -0.25 to 0.25
- w_down: bfloat16 [2, 1536, 576], P('section', 'wsh'), may hold values from -0.15625 to 0.15625
Outputs:
- activations: bfloat16 [2, 2, 2, 4096, 576], P('section', None, 'wsh', 'ctx')
- input_grads: float32 [2, 2, 2, 4096, 576], P('section', None, 'wsh', 'ctx')
- grad_norm_attn: float32 [2, 576], P('section', 'wsh')
- grad_query: float32 [2, 576, 576], P('section', 'wsh')
- grad_key: float32 [2, 576, 192], P('section', 'wsh')
- grad_value: float32 [2, 576, 192], P('section', 'wsh')
- grad_out: float32 [2, 576, 576], P('section', 'wsh')
- grad_norm_mlp: float32 [2, 576], P('section', 'wsh')
- grad_gate: float32 [2, 576, 1536], P('section', 'wsh')
- grad_up: float32 [2, 576, 1536], P('section', 'wsh')
- grad_down: float32 [2, 1536, 576], P('section', 'wsh')
Inputs may be any that keep to these rules, and one draw needn't show every extreme that they name: `positions`: for each micro-batch and sequence the 4096 entries are a permutation of 0 to 4095 made of runs of 64 consecutive numbers, each run starting at a multiple of 64.
All inputs are finite; a program needn't handle non-finite values.
Results may differ from a plain program's by a relative error of at most 0.029.
Values may be sent and summed in bfloat16 or wider, within the bound.
No kernel may reach another device: no remote copies, remote signals or barrier semaphores. Data moves between devices by JAX's collectives and lax.ppermute only.
A program may use at most 128 MiB of HBM per device.

v0:
```python
import jax
import jax.numpy as jnp
from jax import lax
from jax.sharding import PartitionSpec as P

HEADS = 9
KV_HEADS = 3
HEAD_DIM = 64


EPS = 1e-05
NEG = -1e30
BASE = 100000.0


def passed_along(block, axis, distance):
    devices = range(lax.axis_size(axis))
    route = [(i - distance, i) for i in devices if i - distance in devices]
    return lax.ppermute(block, axis, route)


def project(rows, weight):
    return jnp.dot(rows, weight, preferred_element_type=jnp.float32)


def rope_tables(places, width):
    half = width // 2
    freq = BASE ** (-(jnp.arange(half, dtype=jnp.float32) * 2.0 / width))
    angle = places.astype(jnp.float32)[:, None] * freq[None, :]
    return (jnp.cos(angle), jnp.sin(angle))


def rotate(vector, cosine, sine):
    half = vector.shape[-1] // 2
    first = vector[..., :half]
    second = vector[..., half:]
    cosine = cosine[:, None, :]
    sine = sine[:, None, :]
    return jnp.concatenate([first * cosine - second * sine, second * cosine + first * sine], -1)


def rotate_back(grad, cosine, sine):
    half = grad.shape[-1] // 2
    first = grad[..., :half]
    second = grad[..., half:]
    cosine = cosine[:, None, :]
    sine = sine[:, None, :]
    return jnp.concatenate([first * cosine + second * sine, second * cosine - first * sine], -1)


def normalize(hidden):
    inverse = lax.rsqrt(jnp.mean(hidden * hidden, -1, keepdims=True) + EPS)
    return (hidden * inverse, inverse)


def norm_back(grad, normed, inverse):
    return inverse * (grad - normed * jnp.mean(grad * normed, -1, keepdims=True))


def queries_keys(hidden, places, weights):
    count = hidden.shape[0]
    group = HEADS // KV_HEADS
    normed_one, inverse_one = normalize(hidden)
    rows_one = (normed_one * weights[0].astype(jnp.float32)).astype(jnp.bfloat16)
    cosine, sine = rope_tables(places, HEAD_DIM)
    query = rotate(project(rows_one, weights[1]).reshape(count, HEADS, HEAD_DIM), cosine, sine)
    query = query.astype(jnp.bfloat16).reshape(count, KV_HEADS, group, HEAD_DIM)
    keys = rotate(project(rows_one, weights[2]).reshape(count, KV_HEADS, HEAD_DIM), cosine, sine)
    keys = keys.astype(jnp.bfloat16).reshape(count, KV_HEADS * HEAD_DIM)
    values = project(rows_one, weights[3]).astype(jnp.bfloat16)
    return (normed_one, inverse_one, rows_one, cosine, sine, query, keys, values)


def split_blocks(key_all, value_all, places_all):
    length = key_all.shape[0]
    width_block = min(512, length)
    number = length // width_block
    return (
        key_all.reshape(number, width_block, key_all.shape[1]),
        value_all.reshape(number, width_block, value_all.shape[1]),
        places_all.reshape(number, width_block),
    )


def block_scores(query, key_block, places_query, places_key):
    key_heads = key_block.reshape(key_block.shape[0], KV_HEADS, HEAD_DIM)
    scores = jnp.einsum(
        "nkgd,mkd->kgnm", query, key_heads, preferred_element_type=jnp.float32
    ) * HEAD_DIM ** (-0.5)
    allowed = places_key[None, :] <= places_query[:, None]
    return jnp.where(allowed[None, None], scores, NEG)


def attend(query, key_all, value_all, places, places_all):
    blocks = split_blocks(key_all, value_all, places_all)
    count = query.shape[0]
    group = HEADS // KV_HEADS

    def gather_stats(carry, block):
        top, total = carry
        scores = block_scores(query, block[0], places, block[2])
        newtop = jnp.maximum(top, scores.max(-1))
        total = total * jnp.exp(top - newtop) + jnp.exp(scores - newtop[..., None]).sum(-1)
        return ((newtop, total), None)

    start_top = jnp.full((KV_HEADS, group, count), NEG, jnp.float32)
    start_total = jnp.zeros((KV_HEADS, group, count), jnp.float32)
    (top, total), _ = lax.scan(gather_stats, (start_top, start_total), blocks)

    def weigh(accum, block):
        scores = block_scores(query, block[0], places, block[2])
        probs = (jnp.exp(scores - top[..., None]) / total[..., None]).astype(jnp.bfloat16)
        value_heads = block[1].reshape(block[1].shape[0], KV_HEADS, HEAD_DIM)
        return (
            accum
            + jnp.einsum("kgnm,mkd->nkgd", probs, value_heads, preferred_element_type=jnp.float32),
            None,
        )

    accum, _ = lax.scan(weigh, jnp.zeros((count, KV_HEADS, group, HEAD_DIM), jnp.float32), blocks)
    return (accum.reshape(count, HEADS * HEAD_DIM).astype(jnp.bfloat16), top + jnp.log(total))


def attend_back(query, key_all, value_all, places, places_all, log_total, mixed, mixed_grad):
    blocks = split_blocks(key_all, value_all, places_all)
    count = query.shape[0]
    group = HEADS // KV_HEADS
    scale = HEAD_DIM ** (-0.5)
    grad_heads = mixed_grad.reshape(count, KV_HEADS, group, HEAD_DIM)
    mixed_heads = mixed.reshape(count, KV_HEADS, group, HEAD_DIM)
    delta = jnp.sum(grad_heads.astype(jnp.float32) * mixed_heads.astype(jnp.float32), -1).transpose(
        1, 2, 0
    )

    def step(accum, block):
        key_block, value_block, places_block = block
        scores = block_scores(query, key_block, places, places_block)
        probs = jnp.exp(scores - log_total[..., None])
        key_heads = key_block.reshape(key_block.shape[0], KV_HEADS, HEAD_DIM)
        value_heads = value_block.reshape(value_block.shape[0], KV_HEADS, HEAD_DIM)
        prob_grad = jnp.einsum(
            "nkgd,mkd->kgnm", grad_heads, value_heads, preferred_element_type=jnp.float32
        )
        score_grad = (probs * (prob_grad - delta[..., None])).astype(jnp.bfloat16)
        accum = accum + jnp.einsum(
            "kgnm,mkd->nkgd", score_grad, key_heads, preferred_element_type=jnp.float32
        )
        key_term = (
            jnp.einsum("kgnm,nkgd->mkd", score_grad, query, preferred_element_type=jnp.float32)
            * scale
        )
        value_term = jnp.einsum(
            "kgnm,nkgd->mkd",
            probs.astype(jnp.bfloat16),
            grad_heads,
            preferred_element_type=jnp.float32,
        )
        return (
            accum,
            (
                key_term.reshape(key_block.shape[0], KV_HEADS * HEAD_DIM),
                value_term.reshape(key_block.shape[0], KV_HEADS * HEAD_DIM),
            ),
        )

    accum, terms = lax.scan(
        step, jnp.zeros((count, KV_HEADS, group, HEAD_DIM), jnp.float32), blocks
    )
    length = key_all.shape[0]
    return (
        accum * scale,
        terms[0].reshape(length, KV_HEADS * HEAD_DIM),
        terms[1].reshape(length, KV_HEADS * HEAD_DIM),
    )


def layer_forward(entry, places, places_all, weights):
    hidden = entry.astype(jnp.float32)
    normed_one, inverse_one, rows_one, cosine, sine, query, keys, values = queries_keys(
        hidden, places, weights
    )
    key_all, value_all = (
        lax.all_gather(keys, "ctx", axis=0, tiled=True),
        lax.all_gather(values, "ctx", axis=0, tiled=True),
    )
    mixed, log_total = attend(query, key_all, value_all, places, places_all)
    middle = hidden + project(mixed, weights[4])
    normed_two, inverse_two = normalize(middle)
    rows_two = (normed_two * weights[5].astype(jnp.float32)).astype(jnp.bfloat16)
    gate = project(rows_two, weights[6])
    upper = project(rows_two, weights[7])
    inner = (jax.nn.silu(gate) * upper).astype(jnp.bfloat16)
    return (middle + project(inner, weights[8]), log_total, mixed, key_all, value_all)


def layer_backward(entry, places, places_all, weights, log_total, mixed, outgrad):
    count = entry.shape[0]
    hidden = entry.astype(jnp.float32)
    normed_one, inverse_one, rows_one, cosine, sine, query, keys, values = queries_keys(
        hidden, places, weights
    )
    key_all, value_all = (
        lax.all_gather(keys, "ctx", axis=0, tiled=True),
        lax.all_gather(values, "ctx", axis=0, tiled=True),
    )
    middle = hidden + project(mixed, weights[4])
    normed_two, inverse_two = normalize(middle)
    gain_two = weights[5].astype(jnp.float32)
    rows_two = (normed_two * gain_two).astype(jnp.bfloat16)
    gate = project(rows_two, weights[6])
    upper = project(rows_two, weights[7])
    sigma = jax.nn.sigmoid(gate)
    swish = gate * sigma
    inner = (swish * upper).astype(jnp.bfloat16)
    down_grad = outgrad.astype(jnp.bfloat16)
    grad_down = jnp.einsum("nf,nd->fd", inner, down_grad, preferred_element_type=jnp.float32)
    inner_grad = jnp.einsum("nd,fd->nf", down_grad, weights[8], preferred_element_type=jnp.float32)
    gate_grad = (inner_grad * upper * sigma * (1.0 + gate * (1.0 - sigma))).astype(jnp.bfloat16)
    up_grad = (inner_grad * swish).astype(jnp.bfloat16)
    grad_gate = jnp.einsum("nc,nf->cf", rows_two, gate_grad, preferred_element_type=jnp.float32)
    grad_up = jnp.einsum("nc,nf->cf", rows_two, up_grad, preferred_element_type=jnp.float32)
    rows_two_grad = jnp.einsum(
        "nf,cf->nc", gate_grad, weights[6], preferred_element_type=jnp.float32
    ) + jnp.einsum("nf,cf->nc", up_grad, weights[7], preferred_element_type=jnp.float32)
    grad_norm_mlp = jnp.sum(rows_two_grad * normed_two, 0)
    middle_grad = outgrad + norm_back(rows_two_grad * gain_two, normed_two, inverse_two)
    out_grad = middle_grad.astype(jnp.bfloat16)
    grad_out = jnp.einsum("nq,nd->qd", mixed, out_grad, preferred_element_type=jnp.float32)
    mixed_grad = jnp.einsum(
        "nd,qd->nq", out_grad, weights[4], preferred_element_type=jnp.float32
    ).astype(jnp.bfloat16)
    query_sum, key_terms, value_terms = attend_back(
        query, key_all, value_all, places, places_all, log_total, mixed, mixed_grad
    )
    key_sum, value_sum = (
        lax.psum_scatter(
            key_terms.astype(jnp.bfloat16), "ctx", scatter_dimension=0, tiled=True
        ).astype(jnp.float32),
        lax.psum_scatter(
            value_terms.astype(jnp.bfloat16), "ctx", scatter_dimension=0, tiled=True
        ).astype(jnp.float32),
    )
    query_grad = rotate_back(query_sum.reshape(count, HEADS, HEAD_DIM), cosine, sine)
    query_grad = query_grad.reshape(count, HEADS * HEAD_DIM).astype(jnp.bfloat16)
    key_grad = rotate_back(key_sum.reshape(count, KV_HEADS, HEAD_DIM), cosine, sine)
    key_grad = key_grad.reshape(count, KV_HEADS * HEAD_DIM).astype(jnp.bfloat16)
    value_grad = value_sum.astype(jnp.bfloat16)
    grad_query = jnp.einsum("nc,nq->cq", rows_one, query_grad, preferred_element_type=jnp.float32)
    grad_key = jnp.einsum("nc,nq->cq", rows_one, key_grad, preferred_element_type=jnp.float32)
    grad_value = jnp.einsum("nc,nq->cq", rows_one, value_grad, preferred_element_type=jnp.float32)
    rows_one_grad = (
        jnp.einsum("nq,cq->nc", query_grad, weights[1], preferred_element_type=jnp.float32)
        + jnp.einsum("nq,cq->nc", key_grad, weights[2], preferred_element_type=jnp.float32)
        + jnp.einsum("nq,cq->nc", value_grad, weights[3], preferred_element_type=jnp.float32)
    )
    gain_one = weights[0].astype(jnp.float32)
    grad_norm_attn = jnp.sum(rows_one_grad * normed_one, 0)
    hidden_grad = middle_grad + norm_back(rows_one_grad * gain_one, normed_one, inverse_one)
    return (
        hidden_grad,
        (
            grad_norm_attn,
            grad_query,
            grad_key,
            grad_value,
            grad_out,
            grad_norm_mlp,
            grad_gate,
            grad_up,
            grad_down,
        ),
    )


def per_device(
    inputs,
    cotangent,
    positions,
    norm_attn,
    w_query,
    w_key,
    w_value,
    w_out,
    norm_mlp,
    w_gate,
    w_up,
    w_down,
):
    weights = (
        lax.all_gather(norm_attn[0], "wsh", axis=0, tiled=True),
        lax.all_gather(w_query[0], "wsh", axis=0, tiled=True),
        lax.all_gather(w_key[0], "wsh", axis=0, tiled=True),
        lax.all_gather(w_value[0], "wsh", axis=0, tiled=True),
        lax.all_gather(w_out[0], "wsh", axis=0, tiled=True),
        lax.all_gather(norm_mlp[0], "wsh", axis=0, tiled=True),
        lax.all_gather(w_gate[0], "wsh", axis=0, tiled=True),
        lax.all_gather(w_up[0], "wsh", axis=0, tiled=True),
        lax.all_gather(w_down[0], "wsh", axis=0, tiled=True),
    )
    section = lax.axis_index("section")
    first = section == 0
    batches = inputs.shape[0]
    count = inputs.shape[2]
    width = inputs.shape[3]
    places_mine = positions[:, 0, :]
    places_every = lax.all_gather(places_mine, "ctx", axis=1, tiled=True)
    outputs = jnp.zeros((batches, count, width), jnp.bfloat16)
    saved = []
    sent = jnp.zeros((count, width), jnp.bfloat16)
    for tick in range(batches + 1):
        own = inputs[min(tick, batches - 1), 0]
        if tick > 0:
            arrived = passed_along(sent, "section", 1)
            entry = jnp.where(first, own, arrived)
        else:
            entry = own
        batch = tick - section
        index = jnp.clip(batch, 0, batches - 1)
        valid = (batch >= 0) & (batch < batches)
        places = lax.dynamic_index_in_dim(places_mine, index, 0, keepdims=False)
        places_all = lax.dynamic_index_in_dim(places_every, index, 0, keepdims=False)
        result, log_total, mixed, key_all, value_all = layer_forward(
            entry, places, places_all, weights
        )
        sent = result.astype(jnp.bfloat16)
        current = lax.dynamic_index_in_dim(outputs, index, 0, keepdims=False)
        outputs = lax.dynamic_update_index_in_dim(
            outputs, jnp.where(valid, sent, current), index, 0
        )
        saved.append((entry, log_total, mixed, key_all, value_all))
    stacked = jax.tree.map(lambda *items: jnp.stack(items), *saved)
    input_grads = jnp.zeros((batches, count, width), jnp.float32)
    totals = None
    back_sent = jnp.zeros((count, width), jnp.bfloat16)
    for tick in range(batches + 1):
        batch = tick - 1 + section
        index = jnp.clip(batch, 0, batches - 1)
        valid = (batch >= 0) & (batch < batches)
        forward_tick = jnp.clip(tick - 1 + 2 * section, 0, batches)
        picked = jax.tree.map(
            lambda item: lax.dynamic_index_in_dim(item, forward_tick, 0, keepdims=False), stacked
        )
        own = lax.dynamic_index_in_dim(cotangent[:, 0], index, 0, keepdims=False).astype(
            jnp.float32
        )
        if tick > 0:
            arrived = passed_along(back_sent, "section", -1)
            outgrad = jnp.where(first, arrived.astype(jnp.float32), own)
        else:
            outgrad = own
        outgrad = jnp.where(valid, outgrad, 0.0)
        places = lax.dynamic_index_in_dim(places_mine, index, 0, keepdims=False)
        places_all = lax.dynamic_index_in_dim(places_every, index, 0, keepdims=False)
        hidden_grad, layer_grads = layer_backward(
            picked[0], places, places_all, weights, picked[1], picked[2], outgrad
        )
        back_sent = hidden_grad.astype(jnp.bfloat16)
        current = lax.dynamic_index_in_dim(input_grads, index, 0, keepdims=False)
        input_grads = lax.dynamic_update_index_in_dim(
            input_grads, jnp.where(valid, hidden_grad, current), index, 0
        )
        if totals is None:
            totals = layer_grads
        else:
            totals = jax.tree.map(lambda left, right: left + right, totals, layer_grads)
    whole = (
        lax.psum(totals[0].astype(jnp.bfloat16), "ctx").astype(jnp.float32),
        lax.psum(totals[1].astype(jnp.bfloat16), "ctx").astype(jnp.float32),
        lax.psum(totals[2].astype(jnp.bfloat16), "ctx").astype(jnp.float32),
        lax.psum(totals[3].astype(jnp.bfloat16), "ctx").astype(jnp.float32),
        lax.psum(totals[4].astype(jnp.bfloat16), "ctx").astype(jnp.float32),
        lax.psum(totals[5].astype(jnp.bfloat16), "ctx").astype(jnp.float32),
        lax.psum(totals[6].astype(jnp.bfloat16), "ctx").astype(jnp.float32),
        lax.psum(totals[7].astype(jnp.bfloat16), "ctx").astype(jnp.float32),
        lax.psum(totals[8].astype(jnp.bfloat16), "ctx").astype(jnp.float32),
    )
    final = (
        lax.psum_scatter(
            whole[0].astype(jnp.bfloat16), "wsh", scatter_dimension=0, tiled=True
        ).astype(jnp.float32),
        lax.psum_scatter(
            whole[1].astype(jnp.bfloat16), "wsh", scatter_dimension=0, tiled=True
        ).astype(jnp.float32),
        lax.psum_scatter(
            whole[2].astype(jnp.bfloat16), "wsh", scatter_dimension=0, tiled=True
        ).astype(jnp.float32),
        lax.psum_scatter(
            whole[3].astype(jnp.bfloat16), "wsh", scatter_dimension=0, tiled=True
        ).astype(jnp.float32),
        lax.psum_scatter(
            whole[4].astype(jnp.bfloat16), "wsh", scatter_dimension=0, tiled=True
        ).astype(jnp.float32),
        lax.psum_scatter(
            whole[5].astype(jnp.bfloat16), "wsh", scatter_dimension=0, tiled=True
        ).astype(jnp.float32),
        lax.psum_scatter(
            whole[6].astype(jnp.bfloat16), "wsh", scatter_dimension=0, tiled=True
        ).astype(jnp.float32),
        lax.psum_scatter(
            whole[7].astype(jnp.bfloat16), "wsh", scatter_dimension=0, tiled=True
        ).astype(jnp.float32),
        lax.psum_scatter(
            whole[8].astype(jnp.bfloat16), "wsh", scatter_dimension=0, tiled=True
        ).astype(jnp.float32),
    )
    return (
        outputs[None, :, None],
        input_grads[None, :, None],
        final[0][None],
        final[1][None],
        final[2][None],
        final[3][None],
        final[4][None],
        final[5][None],
        final[6][None],
        final[7][None],
        final[8][None],
    )


def solution(mesh):
    placed = (
        P(None, "wsh", "ctx", None),
        P(None, "wsh", "ctx", None),
        P(None, "wsh", "ctx"),
        P("section", "wsh"),
        P("section", "wsh", None),
        P("section", "wsh", None),
        P("section", "wsh", None),
        P("section", "wsh", None),
        P("section", "wsh"),
        P("section", "wsh", None),
        P("section", "wsh", None),
        P("section", "wsh", None),
    )
    return jax.shard_map(
        per_device,
        mesh=mesh,
        in_specs=placed,
        out_specs=(
            P("section", None, "wsh", "ctx", None),
            P("section", None, "wsh", "ctx", None),
            P("section", "wsh"),
            P("section", "wsh", None),
            P("section", "wsh", None),
            P("section", "wsh", None),
            P("section", "wsh", None),
            P("section", "wsh"),
            P("section", "wsh", None),
            P("section", "wsh", None),
            P("section", "wsh", None),
        ),
        check_vma=False,
    )
```

profile of v0, /device:TPU:1, one launch (start us, length us, event | category | flops | bytes accessed | tf_op | source)
XLA Modules:
  0.0 1893.7 jit_solution(5048490600993999892)
XLA Ops:
  7.3 9.1 all-gather.1
  20.2 5.3 all-reduce.7
  28.5 6.4 all-gather.3
  39.8 25.3 %all-gather.2 = s32[2,1,4096]{2,1,0:T(1,128)S(1)} all-gather(s32[2,1,128]{2,1,0:T(1,128)S(1)} %copy-done.206), channel_id=4, replica_groups=mesh['section'=2,'ctx'=32,'wsh'=2] {'ctx'}, dimensions={2}, use_global_device_ids=true | all-gather | bytes 33792 | tf_op jit(solution)/shard_map/all_gather | solution.py:306
  66.4 12.2 all-gather.4
  79.9 11.3 all-gather.5
  94.6 27.5 %all-gather.28.cloned.1.call-done = bf16[4096,192]{0,1:T(8,128)(2,1)} async-done(((bf16[128,192]{0,1:T(8,128)(2,1)}), bf16[4096,192]{0,1:T(8,128)(2,1)}) %all-gather.28.cloned.1.call-update) | async-done | bytes 1572880 | tf_op jit(solution)/shard_map/all_gather | solution.py:183
  124.8 36.0 %while.117 = (s32[]{:T(128)}, f32[3,3,128]{2,1,0:T(4,128)S(1)}, f32[3,3,128]{2,1,0:T(4,128)S(1)}, s32[8,512]{1,0:T(8,128)}, s32[128]{0:T(128)}, /*index=5*/bf16[...) while((s32[]{:T(128)}, f32[3,3,128]{2,1,0:T(4,128)S(1)}, ...), condition=%wide.region_4.5_spmd.clone, body=%wide.region_1.4_spmd.clone.sunk | while | flops 79697536 | bytes 5719160 | solution.py:108
  160.9 42.2 %while.118 = (s32[]{:T(128)}, f32[128,3,3,64]{0,3,2,1:T(8,128)}, bf16[8,512,192]{1,2,0:T(8,128)(2,1)}, s32[8,512]{1,0:T(8,128)}, s32[128]{0:T(128)}, /*index=5*/...) while((s32[]{:T(128)}, f32[128,3,3,64]{0,3,2,1:T(8,128)}, ...), condition=%wide.region_6.7_spmd.clone, body=%wide.region_5.6_spmd.clone.sunk | while | flops 154157056 | bytes 2064007 | solution.py:120
  206.8 18.4 all-gather.52.cloned.1.call-done
  225.9 3.9 bitcast_dynamic-update-slice_fusion.6
  240.8 41.3 %all-gather.30.cloned.1.call-done = bf16[4096,192]{0,1:T(8,128)(2,1)} async-done(((bf16[128,192]{0,1:T(8,128)(2,1)}), bf16[4096,192]{0,1:T(8,128)(2,1)}) %all-gather.30.cloned.1.call-update) | async-done | bytes 1572880 | tf_op jit(solution)/shard_map/all_gather | solution.py:184
  284.7 43.2 %all-gather.32.cloned.1.call-done = bf16[4096,192]{0,1:T(8,128)(2,1)} async-done(((bf16[128,192]{0,1:T(8,128)(2,1)}), bf16[4096,192]{0,1:T(8,128)(2,1)}) %all-gather.32.cloned.1.call-update) | async-done | bytes 1572880 | tf_op jit(solution)/shard_map/all_gather | solution.py:183
  330.7 36.0 %while.119 = (s32[]{:T(128)}, f32[3,3,128]{2,1,0:T(4,128)S(1)}, f32[3,3,128]{2,1,0:T(4,128)S(1)}, s32[8,512]{1,0:T(8,128)}, s32[128]{0:T(128)}, /*index=5*/bf16[...) while((s32[]{:T(128)}, f32[3,3,128]{2,1,0:T(4,128)S(1)}, ...), condition=%wide.region_12.13_spmd.clone, body=%wide.region_9.12_spmd.clone.sunk | while | flops 79697536 | bytes 5719160 | solution.py:108
  366.7 42.1 %while.120 = (s32[]{:T(128)}, f32[128,3,3,64]{0,3,2,1:T(8,128)}, bf16[8,512,192]{1,2,0:T(8,128)(2,1)}, s32[8,512]{1,0:T(8,128)}, s32[128]{0:T(128)}, /*index=5*/...) while((s32[]{:T(128)}, f32[128,3,3,64]{0,3,2,1:T(8,128)}, ...), condition=%wide.region_14.15_spmd.clone, body=%wide.region_13.14_spmd.clone.sunk | while | flops 154157056 | bytes 2064007 | solution.py:120
  412.1 3.6 bitcast_dynamic-update-slice_fusion.5
  436.0 33.2 %all-gather.34.cloned.1.call-done = bf16[4096,192]{0,1:T(8,128)(2,1)} async-done(((bf16[128,192]{0,1:T(8,128)(2,1)}), bf16[4096,192]{0,1:T(8,128)(2,1)}) %all-gather.34.cloned.1.call-update) | async-done | bytes 1572880 | tf_op jit(solution)/shard_map/all_gather | solution.py:184
  471.9 43.3 %all-gather.36.cloned.1.call-done = bf16[4096,192]{0,1:T(8,128)(2,1)} async-done(((bf16[128,192]{0,1:T(8,128)(2,1)}), bf16[4096,192]{0,1:T(8,128)(2,1)}) %all-gather.36.cloned.1.call-update) | async-done | bytes 1572880 | tf_op jit(solution)/shard_map/all_gather | solution.py:183
  517.8 57.6 %while.121 = (s32[]{:T(128)}, f32[3,3,128]{2,1,0:T(4,128)S(1)}, f32[3,3,128]{2,1,0:T(4,128)}, s32[8,512]{1,0:T(8,128)}, s32[128]{0:T(128)}, /*index=5*/bf16[8,51...) while((s32[]{:T(128)}, f32[3,3,128]{2,1,0:T(4,128)S(1)}, ...), condition=%wide.region_20.21_spmd.clone, body=%wide.region_17.20_spmd.clone.sunk | while | flops 79697536 | bytes 6018252 | solution.py:108
  576.2 41.9 %while.122 = (s32[]{:T(128)}, f32[128,3,3,64]{0,3,2,1:T(8,128)}, bf16[8,512,192]{1,2,0:T(8,128)(2,1)}, s32[8,512]{1,0:T(8,128)}, s32[128]{0:T(128)}, /*index=5*/...) while((s32[]{:T(128)}, f32[128,3,3,64]{0,3,2,1:T(8,128)}, ...), condition=%wide.region_22.23_spmd.clone, body=%wide.region_21.22_spmd.clone.sunk | while | flops 154157056 | bytes 2064007 | solution.py:120
  638.6 89.8 %while.123 = (s32[]{:T(128)}, f32[128,3,3,64]{0,3,2,1:T(8,128)}, bf16[8,512,192]{1,2,0:T(8,128)(2,1)}, bf16[8,512,192]{1,2,0:T(8,128)(2,1)}, bf16[8,512,192]{1,2...) while((s32[]{:T(128)}, f32[128,3,3,64]{0,3,2,1:T(8,128)}, ...), condition=%wide.region_29.30_spmd.clone, body=%wide.region_28.29_spmd.clone.sunk | while | flops 383795200 | bytes 25354576 | solution.py:166
  728.5 3.7 copy.201
  732.2 3.7 copy.202
  739.6 69.0 %reduce-scatter.40.cloned.1.call-done = bf16[128,192]{1,0:T(8,128)(2,1)} async-done(((bf16[4096,192]{1,0:T(8,128)(2,1)}), bf16[128,192]{1,0:T(8,128)(2,1)}) %reduce-scatter.40.cloned.1.call-update) | async-done | bytes 49168
  811.5 78.7 %reduce-scatter.42.cloned.1.call-done = bf16[128,192]{1,0:T(8,128)(2,1)} async-done(((bf16[4096,192]{1,0:T(8,128)(2,1)}), bf16[128,192]{1,0:T(8,128)(2,1)}) %reduce-scatter.42.cloned.1.call-update) | async-done | bytes 49168
  912.7 26.3 %all-gather.42.cloned.1.call-done = bf16[4096,192]{0,1:T(8,128)(2,1)} async-done(((bf16[128,192]{0,1:T(8,128)(2,1)}), bf16[4096,192]{0,1:T(8,128)(2,1)}) %all-gather.42.cloned.1.call-update) | async-done | bytes 1572880 | tf_op jit(solution)/shard_map/all_gather | solution.py:203
  941.7 43.1 %all-gather.44.cloned.1.call-done = bf16[4096,192]{0,1:T(8,128)(2,1)} async-done(((bf16[128,192]{0,1:T(8,128)(2,1)}), bf16[4096,192]{0,1:T(8,128)(2,1)}) %all-gather.44.cloned.1.call-update) | async-done | bytes 1572880 | tf_op jit(solution)/shard_map/all_gather | solution.py:204
  990.1 79.7 %while.124 = (s32[]{:T(128)}, f32[128,3,3,64]{0,3,2,1:T(8,128)}, bf16[8,512,192]{1,2,0:T(8,128)(2,1)}, bf16[8,512,192]{1,2,0:T(8,128)(2,1)}, bf16[8,512,192]{1,2...) while((s32[]{:T(128)}, f32[128,3,3,64]{0,3,2,1:T(8,128)}, ...), condition=%wide.region_38.39_spmd.clone, body=%wide.region_37.38_spmd.clone.sunk | while | flops 383795200 | bytes 24006852 | solution.py:166
  1069.8 3.7 copy.203
  1080.9 68.8 %reduce-scatter.44.cloned.1.call-done = bf16[128,192]{1,0:T(8,128)(2,1)} async-done(((bf16[4096,192]{1,0:T(8,128)(2,1)}), bf16[128,192]{1,0:T(8,128)(2,1)}) %reduce-scatter.44.cloned.1.call-update) | async-done | bytes 49168
  1152.7 78.6 %reduce-scatter.46.cloned.1.call-done = bf16[128,192]{1,0:T(8,128)(2,1)} async-done(((bf16[4096,192]{1,0:T(8,128)(2,1)}), bf16[128,192]{1,0:T(8,128)(2,1)}) %reduce-scatter.46.cloned.1.call-update) | async-done | bytes 49168
  1254.0 26.3 %all-gather.46.cloned.1.call-done = bf16[4096,192]{0,1:T(8,128)(2,1)} async-done(((bf16[128,192]{0,1:T(8,128)(2,1)}), bf16[4096,192]{0,1:T(8,128)(2,1)}) %all-gather.46.cloned.1.call-update) | async-done | bytes 1572880 | tf_op jit(solution)/shard_map/all_gather | solution.py:203
  1283.0 43.2 %all-gather.48.cloned.1.call-done = bf16[4096,192]{0,1:T(8,128)(2,1)} async-done(((bf16[128,192]{0,1:T(8,128)(2,1)}), bf16[4096,192]{0,1:T(8,128)(2,1)}) %all-gather.48.cloned.1.call-update) | async-done | bytes 1572880 | tf_op jit(solution)/shard_map/all_gather | solution.py:204
  1331.5 79.6 %while.125 = (s32[]{:T(128)}, f32[128,3,3,64]{0,3,2,1:T(8,128)}, bf16[8,512,192]{1,2,0:T(8,128)(2,1)}, bf16[8,512,192]{1,2,0:T(8,128)(2,1)}, bf16[8,512,192]{1,2...) while((s32[]{:T(128)}, f32[128,3,3,64]{0,3,2,1:T(8,128)}, ...), condition=%wide.region_47.48_spmd.clone, body=%wide.region_46.47_spmd.clone.sunk | while | flops 383795200 | bytes 24006852 | solution.py:166
  1411.1 3.7 copy.205
  1448.1 43.0 %reduce-scatter.48.cloned.1.call-done = bf16[128,192]{1,0:T(8,128)(2,1)} async-done(((bf16[4096,192]{1,0:T(8,128)(2,1)}), bf16[128,192]{1,0:T(8,128)(2,1)}) %reduce-scatter.48.cloned.1.call-update) | async-done | bytes 49168
  1495.4 77.5 %reduce-scatter.50.cloned.1.call-done = bf16[128,192]{1,0:T(8,128)(2,1)} async-done(((bf16[4096,192]{1,0:T(8,128)(2,1)}), bf16[128,192]{1,0:T(8,128)(2,1)}) %reduce-scatter.50.cloned.1.call-update) | async-done | bytes 49168
  1574.8 3.7 fusion.189
  1578.7 18.6 reduce-scatter.32.cloned.1.call-done
  1597.3 34.6 %reduce-scatter.34.cloned.1.call-done = bf16[288,1536]{1,0:T(8,128)(2,1)} async-done(((bf16[576,1536]{1,0:T(8,128)(2,1)}), bf16[288,1536]{1,0:T(8,128)(2,1)}) %reduce-scatter.34.cloned.1.call-update) | async-done | bytes 884752 | tf_op jit(solution)/shard_map/reduce_scatter | solution.py:396
  1631.9 34.6 %reduce-scatter.36.cloned.1.call-done = bf16[288,1536]{1,0:T(8,128)(2,1)} async-done(((bf16[576,1536]{1,0:T(8,128)(2,1)}), bf16[288,1536]{1,0:T(8,128)(2,1)}) %reduce-scatter.36.cloned.1.call-update) | async-done | bytes 884752 | tf_op jit(solution)/shard_map/reduce_scatter | solution.py:399
  1666.5 34.6 %reduce-scatter.38.cloned.1.call-done = bf16[768,576]{0,1:T(8,128)(2,1)} async-done(((bf16[1536,576]{0,1:T(8,128)(2,1)}), bf16[768,576]{0,1:T(8,128)(2,1)}) %reduce-scatter.38.cloned.1.call-update) | async-done | bytes 884752 | tf_op jit(solution)/shard_map/reduce_scatter | solution.py:402
  1701.1 23.2 %reduce-scatter.26.cloned.1.call-done = bf16[288,576]{1,0:T(8,128)(2,1)} async-done(((bf16[576,576]{1,0:T(8,128)(2,1)}), bf16[288,576]{1,0:T(8,128)(2,1)}) %reduce-scatter.26.cloned.1.call-update) | async-done | bytes 331792 | tf_op jit(solution)/shard_map/reduce_scatter | solution.py:381
  1724.3 17.7 reduce-scatter.28.cloned.1.call-done
  1742.1 18.5 reduce-scatter.30.cloned.1.call-done
  1763.7 5.3 all-reduce.6
  1769.1 64.1 %all-reduce.4 = (bf16[288]{0:T(512)(128)(2,1)S(1)}, bf16[288]{0:T(512)(128)(2,1)S(1)}) all-reduce(bf16[288]{0:T(512)(128)(2,1)S(1)} %dynamic-slice.18, bf16[288]{0:T(512)(128)(2,1)S(1)} %dynamic-slice.20), channel_id=1, replica_groups=mesh['section'=2,'ctx'=32,'wsh'=2] {'ctx'}, use_global_device_ids=true, to_apply=%region_54.55 | all-reduce | flops 576 | bytes 2304 | tf_op jit(solution)/shard_map/psum | solution.py:367
  1834.6 41.8 %all-reduce.10.cloned.1.call-done = (bf16[288,576]{1,0:T(8,128)(2,1)}, bf16[288,192]{1,0:T(8,128)(2,1)}, bf16[288,192]{1,0:T(8,128)(2,1)}, bf16[288,576]{1,0:T(8...) async-done(((bf16[288,576]{1,0:T(8,128)(2,1)}, bf16[288,192]{1,0:T(8,128)(2,1)}, bf16[288,192]{1,0:T(8,128)(2,1)}, ...) | async-done | bytes 3538960 | tf_op jit(solution)/shard_map/psum | solution.py:368
  (1433 shorter events, 721.7 us)
Async XLA Ops:
  7.2 84.7 %all-gather.26.cloned.1.call-start = ((), (), s32[]{:S(2)}) async-start(), calls=%async_computation.13 | async-start | bytes 1622016 | tf_op jit(solution)/shard_map/all_gather | solution.py:184
  28.4 93.7 %all-gather.28.cloned.1.call-start = ((), (), s32[]{:S(2)}) async-start(), calls=%async_computation.14 | async-start | bytes 1622016 | tf_op jit(solution)/shard_map/all_gather | solution.py:183
  34.9 389.6 %copy-start.35 = (bf16[1,576,192]{2,1,0:T(8,128)(2,1)}, bf16[1,576,192]{2,1,0:T(8,128)(2,1)S(1)}, u32[]{:S(2)}) copy-start(bf16[1,576,192]{2,1,0:T(8,128)(2,1)S(1)} %all-gather.3) | copy-start | bytes 663556
  37.8 166.9 %all-gather.50.cloned.1.call-start = ((), (), s32[]{:S(2)}) async-start(), calls=%async_computation.25 | async-start | bytes 2654208 | tf_op jit(solution)/shard_map/all_gather | solution.py:296
  38.5 168.2 %all-gather.54.cloned.1.call-start = ((), (), s32[]{:S(2)}) async-start(), calls=%async_computation.27 | async-start | bytes 2654208 | tf_op jit(solution)/shard_map/all_gather | solution.py:298
  39.1 186.1 %all-gather.52.cloned.1.call-start = ((), (), s32[]{:S(2)}) async-start(), calls=%async_computation.26 | async-start | bytes 2654208 | tf_op jit(solution)/shard_map/all_gather | solution.py:297
  39.7 242.3 %all-gather.30.cloned.1.call-start = ((), (), s32[]{:S(2)}) async-start(), calls=%async_computation.15 | async-start | bytes 1622016 | tf_op jit(solution)/shard_map/all_gather | solution.py:184
  91.1 532.5 %copy-start.2 = (bf16[1,576,576]{2,1,0:T(8,128)(2,1)}, bf16[1,576,576]{2,1,0:T(8,128)(2,1)S(1)}, u32[]{:S(2)}) copy-start(bf16[1,576,576]{2,1,0:T(8,128)(2,1)S(1)} %all-gather.5) | copy-start | bytes 1990660
  229.8 4.9 collective-permute-start
  235.8 92.1 %all-gather.32.cloned.1.call-start = ((), (), s32[]{:S(2)}) async-start(), calls=%async_computation.16 | async-start | bytes 1622016 | tf_op jit(solution)/shard_map/all_gather | solution.py:183
  237.0 232.2 %all-gather.34.cloned.1.call-start = ((), (), s32[]{:S(2)}) async-start(), calls=%async_computation.17 | async-start | bytes 1622016 | tf_op jit(solution)/shard_map/all_gather | solution.py:184
  415.7 6.6 collective-permute-start.1
  424.4 90.7 %all-gather.36.cloned.1.call-start = ((), (), s32[]{:S(2)}) async-start(), calls=%async_computation.18 | async-start | bytes 1622016 | tf_op jit(solution)/shard_map/all_gather | solution.py:183
  425.6 193.6 %all-gather.38.cloned.1.call-start = ((), (), s32[]{:S(2)}) async-start(), calls=%async_computation.19 | async-start | bytes 1622016 | tf_op jit(solution)/shard_map/all_gather | solution.py:203
  425.7 466.9 %copy-start.15 = (bf16[3,128,576]{1,2,0:T(8,128)(2,1)}, bf16[3,128,576]{1,2,0:T(8,128)(2,1)S(1)}, u32[]{:S(2)}) copy-start(bf16[3,128,576]{1,2,0:T(8,128)(2,1)S(1)} %pad_maximum_fusion) | copy-start | bytes 1327108
  426.9 203.5 %all-gather.40.cloned.1.call-start = ((), (), s32[]{:S(2)}) async-start(), calls=%async_computation.20 | async-start | bytes 1622016 | tf_op jit(solution)/shard_map/all_gather | solution.py:204
  435.5 373.0 %reduce-scatter.40.cloned.1.call-start = ((), (), s32[]{:S(2)}) async-start(), calls=%async_computation.35 | async-start | bytes 2162688
  732.2 158.0 %reduce-scatter.42.cloned.1.call-start = ((), (), s32[]{:S(2)}) async-start(), calls=%async_computation.36 | async-start | bytes 2162688
  736.0 203.0 %all-gather.42.cloned.1.call-start = ((), (), s32[]{:S(2)}) async-start(), calls=%async_computation.21 | async-start | bytes 1622016 | tf_op jit(solution)/shard_map/all_gather | solution.py:203
  737.0 153.3 %copy-start.56 = (bf16[1,576,192]{2,1,0:T(8,128)(2,1)S(1)}, bf16[1,576,192]{2,1,0:T(8,128)(2,1)}, u32[]{:S(2)}) copy-start(bf16[1,576,192]{2,1,0:T(8,128)(2,1)} %copy-done.53) | copy-start | bytes 663556
  737.0 153.2 %copy-start.187 = (f32[128]{0:T(128)S(1)}, f32[128]{0:T(128)}, u32[]{:S(2)}) copy-start(f32[128]{0:T(128)} %copy-done.185) | copy-start | bytes 1540
  739.6 153.1 %copy-start.67 = (bf16[192,576]{1,0:T(8,128)(2,1)S(1)}, bf16[192,576]{1,0:T(8,128)(2,1)}, u32[]{:S(2)}) copy-start(bf16[192,576]{1,0:T(8,128)(2,1)} %copy-done.65) | copy-start | bytes 663556
  739.6 153.4 %copy-start.158 = (f32[128,32]{0,1:T(8,128)S(1)}, f32[128,32]{0,1:T(8,128)}, u32[]{:S(2)}) copy-start(f32[128,32]{0,1:T(8,128)} %get-tuple-element.1393) | copy-start | bytes 49156
  739.6 153.5 %copy-start.160 = (f32[128,32]{0,1:T(8,128)S(1)}, f32[128,32]{0,1:T(8,128)}, u32[]{:S(2)}) copy-start(f32[128,32]{0,1:T(8,128)} %get-tuple-element.1394) | copy-start | bytes 49156
  810.3 82.7 %copy-start.148 = (bf16[128,3,64]{0,2,1:T(8,128)(2,1)}, bf16[128,3,64]{0,2,1:T(8,128)(2,1)S(1)}, u32[]{:S(2)}) copy-start(bf16[128,3,64]{0,2,1:T(8,128)(2,1)S(1)} %maximum_convert_fusion.3) | copy-start | bytes 147460
  893.7 91.1 %all-gather.44.cloned.1.call-start = ((), (), s32[]{:S(2)}) async-start(), calls=%async_computation.22 | async-start | bytes 1622016 | tf_op jit(solution)/shard_map/all_gather | solution.py:204
  899.4 250.3 %reduce-scatter.44.cloned.1.call-start = ((), (), s32[]{:S(2)}) async-start(), calls=%async_computation.37 | async-start | bytes 2162688
  902.3 6.2 collective-permute-start.2
  1073.5 157.8 %reduce-scatter.46.cloned.1.call-start = ((), (), s32[]{:S(2)}) async-start(), calls=%async_computation.38 | async-start | bytes 2162688
  1077.3 202.9 %all-gather.46.cloned.1.call-start = ((), (), s32[]{:S(2)}) async-start(), calls=%async_computation.23 | async-start | bytes 1622016 | tf_op jit(solution)/shard_map/all_gather | solution.py:203
  1078.3 153.0 %copy-start.17 = (bf16[3,128,576]{1,2,0:T(8,128)(2,1)S(1)}, bf16[3,128,576]{1,2,0:T(8,128)(2,1)}, u32[]{:S(2)}) copy-start(bf16[3,128,576]{1,2,0:T(8,128)(2,1)} %copy-done.15) | copy-start | bytes 1327108
  1078.3 152.9 %copy-start.58 = (bf16[1,576,192]{2,1,0:T(8,128)(2,1)S(1)}, bf16[1,576,192]{2,1,0:T(8,128)(2,1)}, u32[]{:S(2)}) copy-start(bf16[1,576,192]{2,1,0:T(8,128)(2,1)} %copy-done.53) | copy-start | bytes 663556
  1078.3 152.9 %copy-start.189 = (f32[128]{0:T(128)S(1)}, f32[128]{0:T(128)}, u32[]{:S(2)}) copy-start(f32[128]{0:T(128)} %copy-done.188) | copy-start | bytes 1540
  1080.9 152.8 %copy-start.68 = (bf16[192,576]{1,0:T(8,128)(2,1)S(1)}, bf16[192,576]{1,0:T(8,128)(2,1)}, u32[]{:S(2)}) copy-start(bf16[192,576]{1,0:T(8,128)(2,1)} %copy-done.65) | copy-start | bytes 663556
  1080.9 153.4 %copy-start.150 = (f32[128,32]{0,1:T(8,128)S(1)}, f32[128,32]{0,1:T(8,128)}, u32[]{:S(2)}) copy-start(f32[128,32]{0,1:T(8,128)} %get-tuple-element.1363) | copy-start | bytes 49156
  1080.9 153.4 %copy-start.154 = (f32[128,32]{0,1:T(8,128)S(1)}, f32[128,32]{0,1:T(8,128)}, u32[]{:S(2)}) copy-start(f32[128,32]{0,1:T(8,128)} %get-tuple-element.1364) | copy-start | bytes 49156
  1235.0 91.2 %all-gather.48.cloned.1.call-start = ((), (), s32[]{:S(2)}) async-start(), calls=%async_computation.24 | async-start | bytes 1622016 | tf_op jit(solution)/shard_map/all_gather | solution.py:204
  1240.7 250.5 %reduce-scatter.48.cloned.1.call-start = ((), (), s32[]{:S(2)}) async-start(), calls=%async_computation.39 | async-start | bytes 2162688
  1243.4 6.3 collective-permute-start.3
  1414.8 158.0 %reduce-scatter.50.cloned.1.call-start = ((), (), s32[]{:S(2)}) async-start(), calls=%async_computation.40 | async-start | bytes 2162688
  1418.7 178.6 %reduce-scatter.32.cloned.1.call-start = ((), (), s32[]{:S(2)}) async-start(), calls=%async_computation.31 | async-start | bytes 1105920 | tf_op jit(solution)/shard_map/reduce_scatter | solution.py:390
  1421.7 210.2 %reduce-scatter.34.cloned.1.call-start = ((), (), s32[]{:S(2)}) async-start(), calls=%async_computation.32 | async-start | bytes 2654208 | tf_op jit(solution)/shard_map/reduce_scatter | solution.py:396
  1425.7 240.8 %reduce-scatter.36.cloned.1.call-start = ((), (), s32[]{:S(2)}) async-start(), calls=%async_computation.33 | async-start | bytes 2654208 | tf_op jit(solution)/shard_map/reduce_scatter | solution.py:399
  1430.6 270.5 %reduce-scatter.38.cloned.1.call-start = ((), (), s32[]{:S(2)}) async-start(), calls=%async_computation.34 | async-start | bytes 2654208 | tf_op jit(solution)/shard_map/reduce_scatter | solution.py:402
  1437.1 287.2 %reduce-scatter.26.cloned.1.call-start = ((), (), s32[]{:S(2)}) async-start(), calls=%async_computation.28 | async-start | bytes 1105920 | tf_op jit(solution)/shard_map/reduce_scatter | solution.py:381
  1444.8 297.3 %reduce-scatter.28.cloned.1.call-start = ((), (), s32[]{:S(2)}) async-start(), calls=%async_computation.29 | async-start | bytes 442368 | tf_op jit(solution)/shard_map/reduce_scatter | solution.py:384
  1493.8 266.7 %reduce-scatter.30.cloned.1.call-start = ((), (), s32[]{:S(2)}) async-start(), calls=%async_computation.30 | async-start | bytes 442368 | tf_op jit(solution)/shard_map/reduce_scatter | solution.py:387
  1574.7 301.7 %all-reduce.10.cloned.1.call-start = ((), (), s32[]{:S(2)}) async-start(), calls=%async_computation.41 | async-start | bytes 7372800 | tf_op jit(solution)/shard_map/psum | solution.py:368
  (284 other events, 1606.3 us)
Sparse Core Ops, SparseCore 0:
  28.5 47.6 all-gather.25
  78.9 43.1 all-gather.27
  123.8 32.6 all-gather.49
  158.0 32.8 all-gather.53
  192.4 32.7 all-gather.51
  236.0 46.0 all-gather.29
  284.8 43.1 all-gather.31
  424.5 44.5 all-gather.33
  471.9 43.1 all-gather.35
  517.2 43.1 all-gather.37
  562.5 43.1 all-gather.39
  732.3 76.1 reduce-scatter.39
  812.1 78.0 reduce-scatter.41
  893.8 45.1 all-gather.41
  941.6 43.1 all-gather.43
  1073.6 76.0 reduce-scatter.43
  1153.1 78.0 reduce-scatter.45
  1235.1 45.1 all-gather.45
  1283.0 43.1 all-gather.47
  1415.0 76.1 reduce-scatter.47
  1494.7 78.1 reduce-scatter.49
  1575.2 22.0 reduce-scatter.31
  1600.3 31.6 reduce-scatter.33
  1634.8 31.6 reduce-scatter.35
  1669.4 31.6 reduce-scatter.37
  1704.0 20.2 reduce-scatter.25
  1726.6 15.4 reduce-scatter.27
  1745.1 15.4 reduce-scatter.29
  1765.5 110.8 all-reduce.9
where the time goes:
time: 1910 us; the launch traced here: 1890 us
  waiting for transfers between devices  1000 us (52%)
  matrix products  349 us (18%)
  local copies, waits for them, and re-layouts  269 us (14%)
  blocking collectives  139 us (7%)
  other arithmetic  104 us (5%)
    unnamed x35, waiting for transfers between devices  418 us
    dynamic_slice x168, local copies, waits for them, and re-layouts, attend(): (top, total), _ = lax.scan(gather_stats, (start_top, start_total), blocks)  152 us
    all_gather x3, waiting for transfers between devices, layer_forward(): lax.all_gather(keys, 'ctx', axis=0, tiled=True)  114 us
    all_gather x3, waiting for transfers between devices, layer_backward(): lax.all_gather(values, 'ctx', axis=0, tiled=True)  86.4 us
    all_gather x3, waiting for transfers between devices, layer_forward(): lax.all_gather(values, 'ctx', axis=0, tiled=True)  74.5 us
    dot_general x24, matrix products, weigh(): jnp.einsum('kgnm,mkd->nkgd', probs, value_heads, preferred_element_type=j...  64.4 us
    psum x1, blocking collectives, per_device(): lax.psum(totals[0].astype(jnp.bfloat16), 'ctx').astype(jnp.float32)  64.1 us
    dot_general x24, matrix products, step(): jnp.einsum('kgnm,nkgd->mkd', probs.astype(jnp.bfloat16), grad_heads, pref...  56.6 us
  transfers between devices with their start and end apart: 33, of which 28 were waited for; matrix products, arithmetic and copies ran while one was open for 16% of the time, Pallas kernels for 0%

commit v1 on v0

v1 whole, which is shorter than its diff:
```python
import jax
import jax.numpy as jnp
from jax import lax
from jax.experimental import pallas as pl
from jax.experimental.pallas import tpu as pltpu
from jax.sharding import PartitionSpec as P

HEADS = 9
KV_HEADS = 3
GROUP = HEADS // KV_HEADS
HEAD_DIM = 64
D = HEADS * HEAD_DIM
FF = 1536
QKV = D + 2 * KV_HEADS * HEAD_DIM
KVW = 2 * KV_HEADS * HEAD_DIM
SPAN = 128
RUN = 64
LENGTH = 4096
RUNS = LENGTH // RUN
ROWS = GROUP * SPAN
BLOCK = 512
PIECES = LENGTH // BLOCK

EPS = 1e-05
NEG = -1e30
BASE = 100000.0
SCALE = HEAD_DIM ** (-0.5)

BF = jnp.bfloat16
F32 = jnp.float32
VMEM_LIMIT = 56 * 1024 * 1024


def nn(left, right):
    return lax.dot_general(left, right, (((1,), (0,)), ((), ())), preferred_element_type=F32)


def nt(left, right):
    return lax.dot_general(left, right, (((1,), (1,)), ((), ())), preferred_element_type=F32)


def normalize(hidden):
    inverse = lax.rsqrt(jnp.mean(hidden * hidden, -1, keepdims=True) + EPS)
    return hidden * inverse, inverse


def norm_back(grad, normed, inverse):
    return inverse * (grad - normed * jnp.mean(grad * normed, -1, keepdims=True))


def turn(head, cosine, sine):
    half = HEAD_DIM // 2
    first, second = head[:half], head[half:]
    return jnp.concatenate([first * cosine - second * sine, second * cosine + first * sine], 0)


def turn_back(head, cosine, sine):
    half = HEAD_DIM // 2
    first, second = head[:half], head[half:]
    return jnp.concatenate([first * cosine + second * sine, second * cosine - first * sine], 0)


def head_rows(array, head):
    return array[head * HEAD_DIM : (head + 1) * HEAD_DIM]


def group_of(array, group):
    return jnp.concatenate([head_rows(array, group * GROUP + r) for r in range(GROUP)], 1)


def ungroup(parts):
    return jnp.concatenate(
        [parts[g][:, r * SPAN : (r + 1) * SPAN] for g in range(KV_HEADS) for r in range(GROUP)], 0
    )


def attn_rows(hidden, gain):
    normed, inverse = normalize(hidden)
    return normed, inverse, (normed * gain).astype(BF)


def project(rows, w_qkv, cosine, sine, query_ref, kv_ref):
    flat = nn(rows, w_qkv).T
    heads = [turn(head_rows(flat, j), cosine, sine) * SCALE for j in range(HEADS)]
    for g in range(KV_HEADS):
        query_ref[g] = jnp.concatenate(heads[g * GROUP : (g + 1) * GROUP], 1).astype(BF)
    parts = []
    for g in range(KV_HEADS):
        parts.append(turn(head_rows(flat, HEADS + g), cosine, sine))
        parts.append(head_rows(flat, HEADS + KV_HEADS + g))
    kv_ref[...] = jnp.concatenate(parts, 0).T.astype(BF)


def one_hot(first_run, rows):
    lane = lax.broadcasted_iota(jnp.int32, (rows, SPAN), 1)
    run = lax.broadcasted_iota(jnp.int32, (rows, SPAN), 0) // RUN + first_run
    marked = (lane == run) | ((lane >= RUNS) & (lane < RUNS + 3))
    return jnp.where(marked, 1.0, 0.0).astype(BF)


def columns(g):
    return slice(g * SPAN, (g + 1) * SPAN)


def attend(query_ref, kv_refs, bias, triangle):
    zeros = jnp.zeros((HEAD_DIM, ROWS), BF)
    fixed = [jnp.concatenate([query_ref[g], zeros, bias, zeros], 0) for g in range(KV_HEADS)]
    triangle = jnp.concatenate([triangle] * GROUP, 1)
    start = []
    for g in range(KV_HEADS):
        own = kv_refs[0][:SPAN, columns(g)]
        scores = nn(own, fixed[g][:SPAN]) + triangle
        top = jnp.max(scores, 0, keepdims=True)
        probs = jnp.exp(scores - top)
        start += [top, jnp.sum(probs, 0, keepdims=True), nn(own.T[HEAD_DIM:], probs.astype(BF))]

    def step(b, carry):
        skip = SPAN if b == 0 else 0
        marks = one_hot((b * BLOCK + skip) // RUN, BLOCK - skip)
        out = []
        for g in range(KV_HEADS):
            top, total, accum = carry[3 * g : 3 * g + 3]
            block = kv_refs[b][skip:, columns(g)]
            scores = nn(jnp.concatenate([block, marks], 1), fixed[g])
            higher = jnp.maximum(top, jnp.max(scores, 0, keepdims=True))
            probs = jnp.exp(scores - higher)
            fade = jnp.exp(top - higher)
            total = total * fade + jnp.sum(probs, 0, keepdims=True)
            accum = accum * fade + nn(block.T[HEAD_DIM:], probs.astype(BF))
            out += [higher, total, accum]
        return tuple(out)

    done = tuple(start)
    for b in range(PIECES):
        done = step(b, done)
    mixed = [(done[3 * g + 2] / done[3 * g + 1]).astype(BF) for g in range(KV_HEADS)]
    logs = [done[3 * g] + jnp.log(done[3 * g + 1]) for g in range(KV_HEADS)]
    return mixed, logs


def attend_back(query_ref, kv_refs, bias, triangle, mixed, logs, mixed_grad, dkv_refs):
    zeros = jnp.zeros((HEAD_DIM, ROWS), BF)
    row = lax.broadcasted_iota(jnp.int32, (HEAD_DIM, 2 * ROWS), 0)
    triangle = jnp.concatenate([triangle] * GROUP, 1)
    fixed, turned = [], []
    for g in range(KV_HEADS):
        grads = group_of(mixed_grad, g)
        delta = jnp.sum(grads.astype(F32) * mixed[g].astype(F32), 0, keepdims=True)
        less = -jnp.concatenate([logs[g], delta], 1)
        high = less.astype(BF).astype(F32)
        middle = (less - high).astype(BF).astype(F32)
        lowest = less - high - middle
        stats = jnp.where(row == 0, high, jnp.where(row == 1, middle, jnp.where(row == 2, lowest, 0.0)))
        both = jnp.concatenate(
            [jnp.concatenate([query_ref[g], zeros], 1), jnp.concatenate([zeros, grads], 1)], 0
        )
        fixed.append(
            jnp.concatenate([both, jnp.concatenate([bias, zeros], 1), stats.astype(BF)], 0)
        )
        turned.append(both.T)

    def terms(block, marks, g, extra):
        both = nn(jnp.concatenate([block, marks], 1), fixed[g])
        scores = both[:, :ROWS]
        if extra is not None:
            scores = scores + extra
        probs = jnp.exp(scores)
        score_grad = (probs * both[:, ROWS:]).astype(BF)
        kv_terms = nn(jnp.concatenate([score_grad, probs.astype(BF)], 1), turned[g])
        return kv_terms.astype(BF), nn(block.T[:HEAD_DIM], score_grad)

    sums = [jnp.zeros((HEAD_DIM, ROWS), F32)] * KV_HEADS
    for b in range(PIECES):
        skip = SPAN if b == 0 else 0
        marks = one_hot((b * BLOCK + skip) // RUN, BLOCK - skip)
        for g in range(KV_HEADS):
            kv_terms, query_terms = terms(kv_refs[b][skip:, columns(g)], marks, g, None)
            dkv_refs[b][skip:, columns(g)] = kv_terms
            sums[g] = sums[g] + query_terms
    marks = one_hot(2 * RUNS, SPAN)
    for g in range(KV_HEADS):
        kv_terms, query_terms = terms(kv_refs[0][:SPAN, columns(g)], marks, g, triangle)
        dkv_refs[0][:SPAN, columns(g)] = kv_terms
        sums[g] = sums[g] + query_terms
    return ungroup(sums) * SCALE


def feed(middle, gain, w_gate, w_up):
    normed, inverse = normalize(middle)
    rows = (normed * gain).astype(BF)
    return normed, inverse, rows, nn(rows, w_gate), nn(rows, w_up)


def down(inner, w_down):
    half = FF // 2
    return nt(inner[:, :half], w_down[0]) + nt(inner[:, half:], w_down[1])


def feed_back(outgrad, middle, gain, w_gate, w_up, w_down, w_out, parts, refs):
    normed, inverse, rows, gate, upper = parts
    rows_ref, inner_ref, dgate_ref, dup_ref, df_ref, da_ref, gain_ref = refs
    sigma = jax.nn.sigmoid(gate)
    swish = gate * sigma
    df = outgrad.astype(BF)
    inner_grad = jnp.concatenate([nn(df, w_down[i]) for i in range(2)], 1)
    gate_grad = (inner_grad * upper * sigma * (1.0 + gate * (1.0 - sigma))).astype(BF)
    up_grad = (inner_grad * swish).astype(BF)
    rows_grad = nt(gate_grad, w_gate) + nt(up_grad, w_up)
    gain_ref[...] = jnp.sum(rows_grad * normed, 0, keepdims=True)
    middle_grad = outgrad + norm_back(rows_grad * gain, normed, inverse)
    da = middle_grad.astype(BF)
    rows_ref[...] = rows
    inner_ref[...] = (swish * upper).astype(BF)
    dgate_ref[...] = gate_grad
    dup_ref[...] = up_grad
    df_ref[...] = df
    da_ref[:, :D] = da
    da_ref[:, D:] = jnp.zeros((SPAN, 2 * LANES - D), BF)
    return middle_grad, nt(da, w_out).T.astype(BF)


def query_back(dq, cosine, sine):
    parts = [turn_back(head_rows(dq, j), cosine, sine) for j in range(HEADS)]
    return jnp.concatenate(parts, 0).T.astype(BF)


def entry_back(hidden, gain, w_qkv, cosine, sine, query_grad, dkv, middle_grad, rows_ref, dqkv_ref, gain_ref):
    turned = sum(part[...].astype(F32) for part in dkv).T
    parts = [turn_back(head_rows(turned, 2 * g), cosine, sine) for g in range(KV_HEADS)]
    parts += [head_rows(turned, 2 * g + 1) for g in range(KV_HEADS)]
    kv_grad = jnp.concatenate(parts, 0).T.astype(BF)
    grads = jnp.concatenate([query_grad.astype(F32), kv_grad.astype(F32)], 1).astype(BF)
    normed, inverse, rows = attn_rows(hidden, gain)
    rows_grad = nt(grads, w_qkv)
    rows_ref[...] = rows
    dqkv_ref[...] = grads
    gain_ref[...] = jnp.sum(rows_grad * normed, 0, keepdims=True)
    return middle_grad + norm_back(rows_grad * gain, normed, inverse)


VM = pl.BlockSpec(memory_space=pltpu.VMEM)
HBM = pl.BlockSpec(memory_space=pl.ANY)
HALF = D // 2
QUARTER = HALF // 2
A_WIDTH = QKV
B_PART = 1408
B_WIDTH = 4 * B_PART
DOWN_AT = 2 * FF
OUT_AT = 3 * FF


def shape(dims, kind=BF):
    return jax.ShapeDtypeStruct(dims, kind)


def here():
    place = lax.axis_index("ctx")
    return place // 8, lax.rem(place // 2, 4), lax.rem(place, 2)


def start_quarters(layer, sources, copies_of, far_copies_of):
    own, near, far, across, near_twin, far_twin, across_twin = sources
    section, half = lax.axis_index("section"), lax.axis_index("wsh")
    core = here()[2]
    home, away = [], []
    for m, place in enumerate((core, 1 - core)):
        home += copies_of(own, place * QUARTER, True, half, place, m)
        home += far_copies_of(far_twin if m else far, 1 - half, place, 2 + m)
        away += copies_of(near_twin if m else near, 0, False, half, place, m)
        away += copies_of(across_twin if m else across, 0, False, 1 - half, place, 2 + m)

    @pl.when(section == layer)
    def _():
        for copy in home:
            copy.start()

    @pl.when(section != layer)
    def _():
        for copy in away:
            copy.start()

    return away


def rows_at(start, size):
    if isinstance(start, int):
        return pl.ds(start, size)
    return pl.ds(pl.multiple_of(start, 16), size)


def fetch_a(layer, sources, matrix, gains, sems):
    def copies_of(source, first, whole, rows, place, k):
        gain_at = HALF if whole else QUARTER
        out = [
            pltpu.make_async_copy(
                source.at[rows_at(first, QUARTER)],
                matrix.at[rows_at(rows * HALF + place * QUARTER, QUARTER)],
                sems.at[k],
            )
        ]
        if k % 2 == 0:
            out.append(
                pltpu.make_async_copy(
                    source.at[rows_at(gain_at, 16)], gains.at[rows_at(rows * 16, 16)], sems.at[4 + k // 2]
                )
            )
        return out

    def far_copies_of(source, rows, place, k):
        return copies_of(source, 0, False, rows, place, k)

    return start_quarters(layer, sources, copies_of, far_copies_of)


def gain_rows(gains):
    values = gains[...].astype(F32)
    return [
        jnp.concatenate([values[0:1, at : at + HALF], values[16:17, at : at + HALF]], 1) for at in (0, 384)
    ]


def fetch_b(layer, sources, matrix, sems):
    y, x, core = here()

    def copies_of(source, first, whole, rows, place, k):
        return [
            pltpu.make_async_copy(
                source.at[rows_at(first, QUARTER)],
                matrix.at[rows_at(rows * HALF + place * QUARTER, QUARTER)],
                sems.at[k],
            )
        ]

    def far_copies_of(source, rows, place, k):
        at = jnp.where(place == 0, y, x)
        return [
            pltpu.make_async_copy(
                source.at[back],
                matrix.at[
                    rows_at(rows * HALF + place * QUARTER, QUARTER),
                    pl.ds(pl.multiple_of(lax.rem(at + 4 - back, 4) * B_PART, 128), B_PART),
                ],
                sems.at[k],
            )
            for back in range(4)
        ]

    return start_quarters(layer, sources, copies_of, far_copies_of)


def wait_all(copies):
    for copy in copies:
        copy.wait()


A_SCRATCH = [pltpu.VMEM((D, A_WIDTH), BF), pltpu.VMEM((32, A_WIDTH), BF), pltpu.SemaphoreType.DMA((6,))]
B_SCRATCH = [pltpu.VMEM((D, B_WIDTH), BF), pltpu.SemaphoreType.DMA((4,))]


def b_values(matrix):
    halves = [
        jnp.concatenate([matrix[low : low + HALF, at : at + FF // 2] for at in (DOWN_AT, DOWN_AT + FF // 2)], 0)
        for low in (0, HALF)
    ]
    return matrix[:, :FF], matrix[:, FF : 2 * FF], halves, matrix[:, OUT_AT : OUT_AT + D]


def call(kernel, ins, out_shape, scratch, flops, out_spec=VM):
    specs = [spec for spec, arrays in ins for _ in arrays]
    arrays = [array for _, arrays in ins for array in arrays]
    return pl.pallas_call(
        kernel,
        in_specs=specs,
        out_specs=[out_spec] * len(out_shape),
        out_shape=out_shape,
        scratch_shapes=scratch,
        compiler_params=pltpu.CompilerParams(vmem_limit_bytes=VMEM_LIMIT),
        cost_estimate=pl.CostEstimate(flops=flops, bytes_accessed=12_000_000, transcendentals=5_000_000),
    )(*arrays)


QUERY = shape((KV_HEADS, HEAD_DIM, ROWS))
OWN = shape((SPAN, KVW))
TOKENS = shape((SPAN, D))
TURNED = shape((D, SPAN))
TURNED32 = shape((D, SPAN), F32)
TOKENS32 = shape((SPAN, D), F32)
MIXED = shape((KV_HEADS, HEAD_DIM, ROWS))
LOGS = shape((8, ROWS), F32)
GAIN = shape((1, D), F32)
WIDE = shape((SPAN, FF))
FEED_BACK = [TOKENS, WIDE, WIDE, WIDE, TOKENS, shape((SPAN, 768)), GAIN]
PIECE = shape((BLOCK, KVW))


def read_turned(ref):
    return ref[...].astype(F32).T


def open_kernel(x_ref, cos_ref, sin_ref, *refs):
    a, (query_ref, kv_ref), (wqkv, gains, sems) = refs[:7], refs[7:9], refs[9:]
    copies = fetch_a(0, a, wqkv, gains, sems)
    cosine, sine = cos_ref[...], sin_ref[...]
    normed, _ = normalize(read_turned(x_ref))
    wait_all(copies)
    project((normed * gain_rows(gains)[0]).astype(BF), wqkv[...], cosine, sine, query_ref, kv_ref)


def first_kernel(*refs):
    kv_refs, refs = refs[:PIECES], refs[PIECES:]
    (x_ref, query_ref, bias_ref, tri_ref, cos_ref, sin_ref), refs = refs[:6], refs[6:]
    a, b, refs = refs[:7], refs[7:14], refs[14:]
    (act_ref, mixed_ref, logs_ref, middle_ref, query1_ref, kv1_ref), refs = refs[:6], refs[6:]
    a_scr, a0_scr, b_scr = refs[:3], refs[3:6], refs[6:]
    copies_b = fetch_b(0, b, *b_scr)
    copies_a0 = fetch_a(0, a, *a0_scr)
    copies_a = fetch_a(1, a, *a_scr)
    mixed, logs = attend(query_ref, kv_refs, bias_ref[...], tri_ref[...])
    for g in range(KV_HEADS):
        mixed_ref[g] = mixed[g]
        logs_ref[g : g + 1] = logs[g]
    wait_all(copies_b + copies_a0 + copies_a)
    w_gate, w_up, w_down, w_out = b_values(b_scr[0])
    flat = ungroup([m.astype(F32) for m in mixed]).T.astype(BF)
    middle = read_turned(x_ref) + nn(flat, w_out)
    middle_ref[...] = middle
    _, _, _, gate, upper = feed(middle, gain_rows(a0_scr[1])[1], w_gate, w_up)
    inner = (jax.nn.silu(gate) * upper).astype(BF)
    act = (middle + down(inner, w_down)).astype(BF)
    act_ref[...] = act.astype(F32).T.astype(BF)
    _, _, rows = attn_rows(act.astype(F32), gain_rows(a_scr[1])[0])
    project(rows, a_scr[0][...], cos_ref[...], sin_ref[...], query1_ref, kv1_ref)


def second_kernel(*refs):
    kv_refs, refs = refs[:PIECES], refs[PIECES:]
    (x_ref, cot_ref, query_ref, bias_ref, tri_ref, cos_ref, sin_ref), refs = refs[:7], refs[7:]
    a, b, refs = refs[:7], refs[7:14], refs[14:]
    (act_ref, flat_ref, dh2_ref, dq_ref), refs = refs[:4], refs[4:]
    back_refs, refs = refs[:7], refs[7:]
    dkv_refs, refs = refs[:PIECES], refs[PIECES:]
    a_scr, b_scr = refs[:3], refs[3:]
    copies_b = fetch_b(1, b, *b_scr)
    copies_a = fetch_a(1, a, *a_scr)
    bias, triangle = bias_ref[...], tri_ref[...]
    mixed, logs = attend(query_ref, kv_refs, bias, triangle)
    wait_all(copies_b + copies_a)
    w_gate, w_up, w_down, w_out = b_values(b_scr[0])
    flat = ungroup([m.astype(F32) for m in mixed]).T.astype(BF)
    flat_ref[...] = flat
    middle = read_turned(x_ref) + nn(flat, w_out)
    gain = gain_rows(a_scr[1])[1]
    parts = feed(middle, gain, w_gate, w_up)
    dh2, do = feed_back(read_turned(cot_ref), middle, gain, w_gate, w_up, w_down, w_out, parts, back_refs)
    act_ref[...] = (middle + down(back_refs[1][...], w_down)).T.astype(BF)
    dh2_ref[...] = dh2
    dq = attend_back(query_ref, kv_refs, bias, triangle, mixed, logs, do, dkv_refs)
    dq_ref[...] = query_back(dq, cos_ref[...], sin_ref[...])


def third_kernel(*refs):
    kv_refs, refs = refs[:PIECES], refs[PIECES:]
    own_dkv, refs = refs[:4], refs[4:]
    (act_ref, dh2_ref, dq_ref, mixed_ref, logs_ref, middle_ref, query_ref), refs = refs[:7], refs[7:]
    (bias_ref, tri_ref, cos_ref, sin_ref), refs = refs[:4], refs[4:]
    a, b, refs = refs[:7], refs[7:14], refs[14:]
    (grad1_ref, rows1_ref, dqkv1_ref, gain1_ref), refs = refs[:4], refs[4:]
    (flat_ref, dh2_out_ref, dq_out_ref), refs = refs[:3], refs[3:]
    back_refs, refs = refs[:7], refs[7:]
    dkv_refs, refs = refs[:PIECES], refs[PIECES:]
    a_scr, a0_scr, b_scr = refs[:3], refs[3:6], refs[6:]
    copies_a = fetch_a(1, a, *a_scr)
    copies_a0 = fetch_a(0, a, *a0_scr)
    copies_b = fetch_b(0, b, *b_scr)
    cosine, sine = cos_ref[...], sin_ref[...]
    wait_all(copies_a)
    grad = entry_back(
        read_turned(act_ref), gain_rows(a_scr[1])[0], a_scr[0][...], cosine, sine,
        dq_ref[...], own_dkv, dh2_ref[...], rows1_ref, dqkv1_ref, gain1_ref,
    )
    grad1_ref[...] = grad.T
    wait_all(copies_a0 + copies_b)
    w_gate, w_up, w_down, w_out = b_values(b_scr[0])
    mixed = [mixed_ref[g] for g in range(KV_HEADS)]
    logs = [logs_ref[g : g + 1] for g in range(KV_HEADS)]
    flat_ref[...] = ungroup([m.astype(F32) for m in mixed]).T.astype(BF)
    gain = gain_rows(a0_scr[1])[1]
    middle = middle_ref[...]
    parts = feed(middle, gain, w_gate, w_up)
    dh2, do = feed_back(
        grad.astype(BF).astype(F32), middle, gain, w_gate, w_up, w_down, w_out, parts, back_refs
    )
    dh2_out_ref[...] = dh2
    dq = attend_back(query_ref, kv_refs, bias_ref[...], tri_ref[...], mixed, logs, do, dkv_refs)
    dq_out_ref[...] = query_back(dq, cosine, sine)


def close_kernel(*refs):
    own_dkv, refs = refs[:4], refs[4:]
    (x_ref, dh2_ref, dq_ref, cos_ref, sin_ref), refs = refs[:5], refs[5:]
    a, refs = refs[:7], refs[7:]
    (grad_ref, rows_ref, dqkv_ref, gain_ref), a_scr = refs[:4], refs[4:]
    copies = fetch_a(0, a, *a_scr)
    wait_all(copies)
    grad = entry_back(
        read_turned(x_ref), gain_rows(a_scr[1])[0], a_scr[0][...], cos_ref[...], sin_ref[...],
        dq_ref[...], own_dkv, dh2_ref[...], rows_ref, dqkv_ref, gain_ref,
    )
    grad_ref[...] = grad.T


LANES = 384
CHUNKS = 32


def on_the_way(chunk):
    y, x, core = here()
    to_y, to_x, to_core = chunk // 8, chunk // 2 % 4, chunk % 2
    back_y, back_x = lax.rem(y + 4 - to_y, 4), lax.rem(x + 4 - to_x, 4)
    at = back_x * 4 + back_y if to_core == 0 else back_y * 4 + back_x
    return at, core == to_core


def put_chunk(mine_ref, theirs_ref, chunk, value):
    at, stays = on_the_way(chunk)

    @pl.when(stays)
    def _():
        mine_ref[at] = value

    @pl.when(jnp.logical_not(stays))
    def _():
        theirs_ref[at] = value


def send_chunk(held, mine_ref, theirs_ref, sems, chunk):
    at, stays = on_the_way(chunk)
    mine = pltpu.make_async_copy(held.at[chunk], mine_ref.at[at], sems.at[chunk])
    theirs = pltpu.make_async_copy(held.at[chunk], theirs_ref.at[at], sems.at[chunk])

    @pl.when(stays)
    def _():
        mine.start()

    @pl.when(jnp.logical_not(stays))
    def _():
        theirs.start()

    return mine


def feed_grads_kernel(
    flat_ref, da_ref, rows_ref, dgate_ref, dup_ref, inner_ref, df_ref, mine_ref, theirs_ref, held, sems
):
    rows = rows_ref[...].astype(F32).T.astype(BF)
    flat = flat_ref[...].astype(F32).T.astype(BF)
    df = df_ref[...].astype(F32).T.astype(BF)
    copies = []

    def sent(j):
        for r in range(2):
            copies.append(send_chunk(held, mine_ref, theirs_ref, sems, r * 16 + j))

    def put(value, j):
        for half in range(2):
            for r in range(2):
                at = half * HALF + r * QUARTER
                held[r * 16 + j, half] = value[at : at + QUARTER].astype(BF)
        sent(j)

    empty = jnp.zeros((QUARTER, LANES), BF)
    for j in (14, 15):
        for half in range(2):
            for r in range(2):
                held[r * 16 + j, half] = empty
        sent(j)
    for j in range(4):
        lanes = slice(j * LANES, (j + 1) * LANES)
        put(nn(rows, dgate_ref[:, lanes]), j)
        put(nn(rows, dup_ref[:, lanes]), 4 + j)
    for j in range(2):
        for half in range(2):
            at = half * (FF // 2) + j * LANES
            value = nn(df, inner_ref[:, at : at + LANES])
            for top in range(2):
                for r in range(2):
                    line = top * HALF + r * QUARTER
                    held[r * 16 + 8 + 2 * top + j, half] = value[line : line + QUARTER].astype(BF)
        sent(8 + j)
        sent(10 + j)
    put(nn(flat, da_ref[:, :LANES]), 12)
    put(nn(flat, da_ref[:, LANES:]), 13)
    wait_all(copies)


def entry_grads_kernel(*refs):
    mine_ref, theirs_ref = refs[8:]
    values = []
    for layer in range(2):
        rows_ref, dqkv_ref, gain_attn_ref, gain_mlp_ref = refs[4 * layer : 4 * layer + 4]
        rows = rows_ref[...].astype(F32).T.astype(BF)
        value = nn(rows, dqkv_ref[...])
        gains = jnp.concatenate(
            [gain_attn_ref[...], gain_mlp_ref[...], jnp.zeros((HEAD_DIM - 2, D), F32)], 0
        ).T
        values.append(jnp.concatenate([value, gains], 1).astype(BF))
    for r in range(2):
        for j in range(16):
            lanes = slice(j * HEAD_DIM, (j + 1) * HEAD_DIM)
            parts = [
                value[half * HALF + r * QUARTER : half * HALF + (r + 1) * QUARTER, lanes]
                for value in values
                for half in range(2)
            ]
            put_chunk(mine_ref, theirs_ref, r * 16 + j, jnp.concatenate(parts, 1))


def unpack_kernel(*refs):
    came, refs = refs[:8], refs[8:]
    (norms_ref, query_ref, key_ref, value_ref, out_ref, gate_ref, up_ref, down_ref), (held,) = refs[:8], refs[8:]
    y, x, core = here()
    for piece in range(8):
        which = core if piece < 4 else 1 - core
        k2 = piece % 4
        for k1 in range(4):
            back_y = jnp.where(which == 0, k1, k2)
            back_x = jnp.where(which == 0, k2, k1)
            chunk = lax.rem(y + 4 - back_y, 4) * 8 + lax.rem(x + 4 - back_x, 4) * 2 + which
            held[chunk] = came[piece][k1]
    for r in range(2):
        rows = slice(r * QUARTER, (r + 1) * QUARTER)

        def block(j):
            return held[r * 16 + j, :, :LANES].astype(F32)

        def head(j):
            return held[r * 16 + j, :, LANES:].astype(F32)

        for j in range(4):
            lanes = slice(j * LANES, (j + 1) * LANES)
            gate_ref[rows, lanes] = block(j)
            up_ref[rows, lanes] = block(4 + j)
        for j in range(2):
            lanes = slice(j * LANES, (j + 1) * LANES)
            for top in range(2):
                down_ref[top * HALF + r * QUARTER : top * HALF + (r + 1) * QUARTER, lanes] = block(8 + 2 * top + j)
        out_ref[rows] = jnp.concatenate([block(12), block(13)[:, : D - LANES]], 1)
        query_ref[rows] = jnp.concatenate([head(j) for j in range(HEADS)], 1)
        key_ref[rows] = jnp.concatenate([head(HEADS + j) for j in range(KV_HEADS)], 1)
        value_ref[rows] = jnp.concatenate([head(HEADS + KV_HEADS + j) for j in range(KV_HEADS)], 1)
    turned = jnp.concatenate([held[r * 16 + 15, :, LANES:].astype(F32).T for r in range(2)], 1)
    norms_ref[...] = turned[:8]


def routes(axes_size):
    def turn_of(i, along_y, k):
        core, x, y = i % 2, i // 2 % 4, i // 8
        if along_y:
            y = (y + k) % 4
        else:
            x = (x + k) % 4
        return y * 8 + x * 2 + core

    def first(k):
        return [(i, turn_of(i, i % 2 == 0, k)) for i in range(axes_size)]

    def second(k):
        return [(i, turn_of(i, i % 2 == 1, k)) for i in range(axes_size)]

    return first, second, [(i, i ^ 1) for i in range(axes_size)]


def per_device(
    inputs, cotangent, positions, norm_attn, w_query, w_key, w_value, w_out, norm_mlp, w_gate, w_up, w_down
):
    section = lax.axis_index("section")
    place = lax.axis_index("ctx")
    core = place % 2
    first, second, swap = routes(lax.axis_size("ctx"))

    def hop(block, route):
        return lax.ppermute(block, "ctx", route)

    def along_z(block, flip):
        return lax.ppermute(block, ("section", "wsh"), [(i, i ^ flip) for i in range(4)])

    spots = lax.dynamic_index_in_dim(positions, section, 0, keepdims=False)[0]
    gains = jnp.concatenate(
        [norm_attn, jnp.zeros((1, 96), BF), norm_mlp, jnp.zeros((1, A_WIDTH - 384 - HALF), BF)], 1
    )
    gains = jnp.concatenate([gains, jnp.zeros((15, A_WIDTH), BF)], 0)
    own_a = jnp.concatenate([w_query[0], w_key[0], w_value[0]], 1)
    half_a = jnp.concatenate([lax.dynamic_slice_in_dim(own_a, core * QUARTER, QUARTER, 0), gains], 0)
    own_a = jnp.concatenate([own_a, gains], 0)
    turned = w_down[0].T
    own_b = jnp.concatenate(
        [w_gate[0], w_up[0], turned[:HALF], turned[HALF:], w_out[0], jnp.zeros((HALF, B_WIDTH - OUT_AT - D), BF)], 1
    )
    half_b = lax.dynamic_slice_in_dim(own_b, core * QUARTER, QUARTER, 0)

    came = [along_z(half_a, flip) for flip in (2, 1, 3)]
    a = [own_a] + came + [hop(block, swap) for block in came]
    starts = lax.all_gather(spots[::RUN], "ctx", axis=0, tiled=True)

    x = lax.dynamic_index_in_dim(inputs, section, 0, keepdims=False)[0].T
    cot = lax.dynamic_index_in_dim(cotangent, section, 0, keepdims=False)[0].T
    freq = BASE ** (-(jnp.arange(HEAD_DIM // 2, dtype=F32) * 2.0 / HEAD_DIM))
    angle = freq[:, None] * spots.astype(F32)[None, :]
    cosine, sine = jnp.cos(angle), jnp.sin(angle)
    triangle = jnp.where(spots[:, None] <= spots[None, :], 0.0, NEG).astype(F32)

    k1, k2 = jnp.arange(4)[None, :], jnp.arange(4)[:, None]
    y, x_at = place // 8, place // 2 % 4

    def origin(which):
        back_y = jnp.where(which == 0, k1, k2)
        back_x = jnp.where(which == 0, k2, k1)
        return ((y - back_y) % 4 * 8 + (x_at - back_x) % 4 * 2 + which).reshape(16)

    order = jnp.concatenate([origin(core), origin(1 - core)])
    picked = order[:, None] == jnp.arange(CHUNKS)[None, :]
    starts = jnp.sum(jnp.where(picked[:, :, None], starts.reshape(1, CHUNKS, 2), 0), 1).reshape(RUNS)
    open_run = (starts[:, None] < (spots - spots % RUN)[None, :]) & (jnp.arange(RUNS)[:, None] > 1)
    bias = jnp.tile(jnp.where(open_run, 0.0, NEG), (1, GROUP)).astype(BF)

    def gathered(own):
        four = jnp.concatenate([own] + [hop(own, first(k)) for k in (1, 2, 3)], 0)
        mine = [four] + [hop(four, second(k)) for k in (1, 2, 3)]
        return mine + [hop(piece, swap) for piece in mine]

    def summed(pieces):
        def add(*parts):
            return sum(part.astype(F32) for part in parts).astype(BF)

        mine = [add(pieces[k], hop(pieces[4 + k], swap)) for k in range(4)]
        four = add(mine[0], *[hop(mine[k], second(-k)) for k in (1, 2, 3)])
        parts = [four[k * SPAN : (k + 1) * SPAN] for k in range(4)]
        return [parts[0]] + [hop(parts[k], first(-k)) for k in (1, 2, 3)]

    def ring(block):
        return jnp.stack([block] + [hop(block, first(k)) for k in (1, 2, 3)])

    half_b, *_ = lax.optimization_barrier((half_b, *a[1:4]))
    near, across = along_z(half_b, 2), along_z(half_b, 3)
    ring_place = jnp.where(core == 0, y, x_at)
    part = lax.dynamic_slice_in_dim(half_b, ring_place * B_PART, B_PART, 1)
    far = ring(along_z(part, 1))
    b = [own_b, near, far, across] + [hop(block, swap) for block in (near, far, across)]
    x, bias = lax.optimization_barrier((x, bias))
    query0, own0 = call(
        open_kernel, [(VM, [x, cosine, sine]), (HBM, a)], [QUERY, OWN], A_SCRATCH, 10**8
    )
    all0 = gathered(own0)
    act0, mixed0, logs0, middle0, query1, own1 = call(
        first_kernel,
        [(VM, all0 + [x, query0, bias, triangle, cosine, sine]), (HBM, a + b)],
        [TURNED, MIXED, LOGS, TOKENS32, QUERY, OWN],
        A_SCRATCH + A_SCRATCH + B_SCRATCH,
        2 * 10**9,
    )
    all1 = gathered(own1)
    act1, flat, dh2, dq, rows, inner, dgate, dup, df, da, gain_mlp1, *dkv = call(
        second_kernel,
        [(VM, all1 + [act0, cot, query1, bias, triangle, cosine, sine]), (HBM, a + b)],
        [TURNED, TOKENS, TOKENS32, TOKENS] + FEED_BACK + [PIECE] * PIECES,
        A_SCRATCH + B_SCRATCH,
        7 * 10**9,
    )
    def add(*parts):
        return sum(part.astype(F32) for part in parts).astype(BF)

    def to_cores(mine, theirs):
        came = hop(theirs, swap)
        return [add(mine[4 * k : 4 * k + 4], came[4 * k : 4 * k + 4]) for k in range(4)]

    def to_rings(sets):
        came = [hop(sets[k], second(-k)) for k in (1, 2, 3)]
        return [add(sets[0][k], *[block[k] for block in came]) for k in range(4)]

    def to_place(blocks):
        return add(blocks[0], *[hop(blocks[k], first(-k)) for k in (1, 2, 3)])

    FEED_SCRATCH = [pltpu.VMEM((CHUNKS, 2, QUARTER, LANES), BF), pltpu.SemaphoreType.DMA((CHUNKS,))]
    FEEDS = [shape((16, 2, QUARTER, LANES))] * 2
    ENTRIES = [shape((16, QUARTER, 4 * HEAD_DIM))] * 2
    own_dkv = summed(dkv)
    feed1 = call(feed_grads_kernel, [(VM, [flat, da, rows, dgate, dup, inner, df])], FEEDS, FEED_SCRATCH, 10**9, HBM)
    feed1 = to_cores(*feed1)
    dq, *feed1 = lax.optimization_barrier((dq, *feed1))
    feed1 = to_rings(feed1)
    (
        grad1, rows_in1, dqkv1, gain_attn1,
        flat, dh2, dq, rows, inner, dgate, dup, df, da, gain_mlp0, *dkv,
    ) = call(
        third_kernel,
        [
            (VM, all0 + own_dkv + [act0, dh2, dq, mixed0, logs0, middle0, query0]),
            (VM, [bias, triangle, cosine, sine]),
            (HBM, a + b),
        ],
        [TURNED32, TOKENS, shape((SPAN, QKV)), GAIN]
        + [TOKENS, TOKENS32, TOKENS]
        + FEED_BACK
        + [PIECE] * PIECES,
        A_SCRATCH + A_SCRATCH + B_SCRATCH,
        6 * 10**9,
    )
    own_dkv = summed(dkv)
    feed1 = to_place(feed1)
    feed0 = call(feed_grads_kernel, [(VM, [flat, da, rows, dgate, dup, inner, df])], FEEDS, FEED_SCRATCH, 10**9, HBM)
    feed0 = to_place(to_rings(to_cores(*feed0)))
    grad0, rows_in0, dqkv0, gain_attn0 = call(
        close_kernel,
        [(VM, own_dkv + [x, dh2, dq, cosine, sine]), (HBM, a)],
        [TURNED32, TOKENS, shape((SPAN, QKV)), GAIN],
        A_SCRATCH,
        10**8,
    )
    entries = call(
        entry_grads_kernel,
        [(VM, [rows_in0, dqkv0, gain_attn0, gain_mlp0, rows_in1, dqkv1, gain_attn1, gain_mlp1])],
        ENTRIES,
        [],
        10**8,
    )
    entries = to_place(to_rings(to_cores(*entries)))

    entries = entries.reshape(QUARTER, 2, 2, HEAD_DIM).transpose(1, 2, 0, 3)
    every = jnp.concatenate([jnp.stack([feed0, feed1]), entries], -1).reshape(4, QUARTER, LANES + HEAD_DIM)
    spot = section * 2 + lax.axis_index("wsh")

    def chunk(flip):
        return lax.dynamic_index_in_dim(every, spot ^ flip, 0, keepdims=False)

    total = add(chunk(0), *[along_z(chunk(flip), flip) for flip in (1, 2, 3)])
    four = jnp.stack([total] + [hop(total, first(k)) for k in (1, 2, 3)])
    mine = [four] + [hop(four, second(k)) for k in (1, 2, 3)]
    came = mine + [hop(piece, swap) for piece in mine]
    norms, g_query, g_key, g_value, g_out, g_gate, g_up, g_down = call(
        unpack_kernel,
        [(VM, came)],
        [
            shape((8, HALF), F32), shape((HALF, D), F32), shape((HALF, KVW // 2), F32), shape((HALF, KVW // 2), F32),
            shape((HALF, D), F32), shape((HALF, FF), F32), shape((HALF, FF), F32), shape((D, FF // 2), F32),
        ],
        [pltpu.VMEM((CHUNKS, QUARTER, LANES + HEAD_DIM), BF)],
        10**8,
    )

    def exchanged(own, other):
        kept = jnp.where(section == 0, own, other)
        sent = jnp.where(section == 0, other, own)
        came = lax.ppermute(sent, "section", [(0, 1), (1, 0)])
        return jnp.where(section == 0, jnp.stack([kept, came]), jnp.stack([came, kept]))

    acts = exchanged(act0, act1)
    grads = exchanged(grad0, grad1)
    return (
        acts.swapaxes(1, 2)[None, :, None],
        grads.swapaxes(1, 2)[None, :, None],
        norms[0:1],
        g_query[None],
        g_key[None],
        g_value[None],
        g_out[None],
        norms[1:2],
        g_gate[None],
        g_up[None],
        g_down.T[None],
    )


def solution(mesh):
    placed = (
        P(None, "wsh", "ctx", None),
        P(None, "wsh", "ctx", None),
        P(None, "wsh", "ctx"),
        P("section", "wsh"),
        P("section", "wsh", None),
        P("section", "wsh", None),
        P("section", "wsh", None),
        P("section", "wsh", None),
        P("section", "wsh"),
        P("section", "wsh", None),
        P("section", "wsh", None),
        P("section", "wsh", None),
    )
    return jax.shard_map(
        per_device,
        mesh=mesh,
        in_specs=placed,
        out_specs=(
            P("section", None, "wsh", "ctx", None),
            P("section", None, "wsh", "ctx", None),
            P("section", "wsh"),
            P("section", "wsh", None),
            P("section", "wsh", None),
            P("section", "wsh", None),
            P("section", "wsh", None),
            P("section", "wsh"),
            P("section", "wsh", None),
            P("section", "wsh", None),
            P("section", "wsh", None),
        ),
        check_vma=False,
    )
```

time: 1910 us -> 457 us (0.24)
  waiting for transfers between devices: 1000 us -> 162 us
  matrix products: 349 us -> 0 us
  local copies, waits for them, and re-layouts: 269 us -> 27.6 us
  blocking collectives: 139 us -> 15.4 us
  Pallas kernels: 0 us -> 103 us
  starting transfers between devices: 11 us -> 113 us
  other arithmetic: 104 us -> 25.1 us
    unnamed x35 -> x0, waiting for transfers between devices: 418 us -> none
    dot_general x246 -> x0, matrix products: 349 us -> none  [the longest x24 64.4 us: weigh(): jnp.einsum('kgnm,mkd->nkgd', probs, value_heads, preferred_element_type=j...]
    all_gather x15 -> x0, waiting for transfers between devices: 346 us -> none  [the longest x3 114 us: layer_forward(): lax.all_gather(keys, 'ctx', axis=0, tiled=True)]
    reduce_scatter x7 -> x0, waiting for transfers between devices: 182 us -> none  [the longest x1 34.6 us: per_device(): lax.psum_scatter(whole[6].astype(jnp.bfloat16), 'wsh', scatter_dimension=...]
    dynamic_slice x172 -> x2, local copies, waits for them, and re-layouts: 154 us -> 2.47 us  [the longest x1 1.44 us: per_device(): half_b = lax.dynamic_slice_in_dim(own_b, core * QUARTER, QUARTER, 0)]
    ppermute x4 -> x91, waiting for transfers between devices: 12.7 us -> 162 us  [the longest x80 125 us: hop(): return lax.ppermute(block, 'ctx', route)]
    ppermute x4 -> x91, starting transfers between devices: 8.78 us -> 113 us  [the longest x80 98.4 us: hop(): return lax.ppermute(block, 'ctx', route)]
    pallas_call x0 -> x9, Pallas kernels: none -> 103 us  [call(): pl.pallas_call(kernel, in_specs=specs, out_specs=[out_spec] * len(out_sha...]
  transfers between devices with their start and end apart: 33 -> 91, of which waited for: 28 -> 40; matrix products, arithmetic and copies ran while one was open for 16% -> 8% of each run, Pallas kernels for 0% -> 3%
where the time goes in v1:
time: 457 us; the launch traced here: 448 us
  waiting for transfers between devices  162 us (35%)
  starting transfers between devices  113 us (25%)
  Pallas kernels  103 us (23%)
  local copies, waits for them, and re-layouts  27.6 us (6%)
  other arithmetic  25.1 us (5%)
  blocking collectives  15.4 us (3%)
    ppermute x80, waiting for transfers between devices, hop(): return lax.ppermute(block, 'ctx', route)  125 us
    pallas_call x9, Pallas kernels, call(): pl.pallas_call(kernel, in_specs=specs, out_specs=[out_spec] * len(out_sha...  103 us
    ppermute x80, starting transfers between devices, hop(): return lax.ppermute(block, 'ctx', route)  98.4 us
    ppermute x9, waiting for transfers between devices, along_z(): lax.ppermute(block, ('section', 'wsh'), [(i, i ^ flip) for i in range(4)])  29.6 us
    unnamed x1, blocking collectives  15.4 us
    ppermute x9, starting transfers between devices, along_z(): lax.ppermute(block, ('section', 'wsh'), [(i, i ^ flip) for i in range(4)])  14.1 us
    unnamed x168, local copies, waits for them, and re-layouts  13.2 us
    convert_element_type x13, other arithmetic, add(): return sum((part.astype(F32) for part in parts)).astype(BF)  9.4 us
  transfers between devices with their start and end apart: 91, of which 40 were waited for; matrix products, arithmetic and copies ran while one was open for 8% of the time, Pallas kernels for 3%

profile of v1, /device:TPU:1, one launch (start us, length us, event | category | flops | bytes accessed | tf_op | source)
XLA Modules:
  0.0 448.3 jit_solution(6608224008424906242)
XLA Ops:
  3.5 2.5 collective-permute-start
  6.0 3.3 collective-permute-start.1
  11.4 15.4 %all-reduce = s32[64]{0:T(128)S(1)} all-reduce(s32[64]{0:T(128)S(1)} %dynamic-update-slice), channel_id=1, replica_groups=mesh['section'=2,'ctx'=32,'wsh'=2] {'ctx'}, use_global_device_ids=true, to_apply=%add | all-reduce | flops 64 | bytes 512
  30.0 4.7 %concatenate.36.refs_21_.refs_22_.refs_30_ = bf16[288,5632]{1,0:T(8,128)(2,1)S(1)} concatenate(bf16[288,1536]{1,0:T(8,128)(2,1)} %bitcast.119, bf16[288,1536]{1,0:T(8,128)(2,1)} %bitcast.120, bf16[288,768]{1,0:T(8,128)(2,1)} %get-tuple-element.218, bf16[288,768]{1,0:T(8,128)(2,1)} %get-tuple-element.217, bf16[288,576]{1,0:T(8,128)(2,1)} %bitcast.131, ...), dimensions={1} | concatenate | bytes 6488064 | tf_op jit(solution)/shard_map/concatenate | solution.py:696
  37.1 3.0 collective-permute-start.21
  41.5 3.0 collective-permute-start.3
  52.0 3.5 shard_map.203
  57.2 25.6 %collective-permute-done.17 = bf16[144,1408]{1,0:T(8,128)(2,1)S(1)} collective-permute-done((bf16[144,1408]{1,0:T(8,128)(2,1)S(1)}, bf16[144,1408]{1,0:T(8,128)(2,1)S(1)}, u32[]{:S(2)}, u32[]{:S(2)}) %collective-permute-start.17) | collective-permute-done | bytes 405536 | tf_op jit(solution)/shard_map/ppermute | solution.py:685
  85.5 4.4 collective-permute-done.20
  91.4 4.3 collective-permute-done.18
  96.0 4.8 %collective-permute-start.23 = (bf16[4,144,1408]{2,1,0:T(8,128)(2,1)S(1)}, bf16[4,144,1408]{2,1,0:T(8,128)(2,1)S(1)}, u32[]{:S(2)}, u32[]{:S(2)}) collective-permute-start(bf16[4,144,1408]{2,1,0:T(8,128)(2,1)S(1)} %pad_maximum_fusion.refs_23_.refs_24_.refs_32_), channel_id=1, source_target_pairs={{0,2},{2,0},{4,6},{6,4},{8,10},{10,8},{12,14},{14,12},{16,18},{18,... | collective-permute-start | bytes 4866056 | tf_op jit(solution)/shard_map/ppermute | solution.py:682
  103.3 10.4 %collective-permute-done.9.refs_1_ = bf16[512,384]{1,0:T(8,128)(2,1)S(1)} collective-permute-done((bf16[512,384]{1,0:T(8,128)(2,1)S(1)}, bf16[512,384]{1,0:T(8,128)(2,1)S(1)}, u32[]{:S(2)}, u32[]{:S(2)}) %collective-permute-start.9) | collective-permute-done | bytes 393248 | tf_op jit(solution)/shard_map/ppermute | solution.py:682
  114.9 5.9 %collective-permute-done.11.refs_3_ = bf16[512,384]{1,0:T(8,128)(2,1)S(1)} collective-permute-done((bf16[512,384]{1,0:T(8,128)(2,1)S(1)}, bf16[512,384]{1,0:T(8,128)(2,1)S(1)}, u32[]{:S(2)}, u32[]{:S(2)}) %collective-permute-start.11) | collective-permute-done | bytes 393248 | tf_op jit(solution)/shard_map/ppermute | solution.py:682
  128.6 15.5 %shard_map.204 = (bf16[576,128]{1,0:T(8,128)(2,1)}, bf16[3,64,384]{2,1,0:T(8,128)(2,1)}, f32[8,384]{1,0:T(8,128)}, f32[128,576]{1,0:T(8,128)}, bf16[3,64,384]{2,1,0:T(8,128)(2,1)}, /*index=5*/bf16[128,384]{1,0:T(8,128)(2,1)}) custom-call(bf16[512,384]{1,0:T(8,128)(2,1)} %copy-done.13, bf16[512,384]{1,0:T(8,128)(2,1)} %copy-done.23, ...), custom_call_target="tpu_custom_call" | custom-call | flops 2000000000 | bytes 12000000 | tf_op jit(solution)/shard_map/pallas_call | solution.py:371
  155.9 7.7 %collective-permute-done.28.refs_1_ = bf16[512,384]{1,0:T(8,128)(2,1)S(1)} collective-permute-done((bf16[512,384]{1,0:T(8,128)(2,1)S(1)}, bf16[512,384]{1,0:T(8,128)(2,1)S(1)}, u32[]{:S(2)}, u32[]{:S(2)}) %collective-permute-start.28) | collective-permute-done | bytes 393248 | tf_op jit(solution)/shard_map/ppermute | solution.py:682
  169.1 32.6 %shard_map.205 = (bf16[576,128]{1,0:T(8,128)(2,1)}, bf16[128,576]{1,0:T(8,128)(2,1)}, f32[128,576]{1,0:T(8,128)}, bf16[128,576]{1,0:T(8,128)(2,1)}, bf16[128,576...) custom-call(bf16[512,384]{1,0:T(8,128)(2,1)} %copy-done.44, ...), custom_call_target="tpu_custom_call" | custom-call | flops 7000000000 | bytes 12000000 | tf_op jit(solution)/shard_map/pallas_call | solution.py:371
  201.8 4.9 %shard_map.206 = (bf16[16,2,144,384]{3,2,1,0:T(8,128)(2,1)}, bf16[16,2,144,384]{3,2,1,0:T(8,128)(2,1)}) custom-call(bf16[128,576]{1,0:T(8,128)(2,1)} %get-tuple-element.105.flat_ref, bf16[128,768]{1,0:T(8,128)(2,1)} %get-tuple-element.106.da_ref, bf16[128,576]{1,0:T(8,128)(2,1)} %get-tuple-element.107.rows_ref, ...), custom_call_target="tpu_custom_call" | custom-call | flops 1000000000 | bytes 12000000 | tf_op jit(solution)/shard_map/pallas_call | solution.py:371
  208.2 4.7 %collective-permute-done.41 = bf16[512,384]{1,0:T(8,128)(2,1)S(1)} collective-permute-done((bf16[512,384]{1,0:T(8,128)(2,1)S(1)}, bf16[512,384]{1,0:T(8,128)(2,1)S(1)}, u32[]{:S(2)}, u32[]{:S(2)}) %collective-permute-start.41) | collective-permute-done | bytes 393248 | tf_op jit(solution)/shard_map/ppermute | solution.py:682
  214.9 2.7 collective-permute-start.40
  217.9 3.8 collective-permute-done.42
  221.7 5.1 %collective-permute-done.40 = bf16[512,384]{1,0:T(8,128)(2,1)S(1)} collective-permute-done((bf16[512,384]{1,0:T(8,128)(2,1)S(1)}, bf16[512,384]{1,0:T(8,128)(2,1)S(1)}, u32[]{:S(2)}, u32[]{:S(2)}) %collective-permute-start.40) | collective-permute-done | bytes 393248 | tf_op jit(solution)/shard_map/ppermute | solution.py:682
  236.0 24.8 %shard_map.207 = (f32[576,128]{1,0:T(8,128)}, bf16[128,576]{1,0:T(8,128)(2,1)}, bf16[128,960]{1,0:T(8,128)(2,1)}, f32[1,576]{1,0:T(1,128)}, bf16[128,576]{1,0:T(...) custom-call(bf16[512,384]{1,0:T(8,128)(2,1)} %copy-done.13, ...), custom_call_target="tpu_custom_call" | custom-call | flops 6000000000 | bytes 12000000 | tf_op jit(solution)/shard_map/pallas_call | solution.py:371
  260.8 4.8 %shard_map.209 = (bf16[16,2,144,384]{3,2,1,0:T(8,128)(2,1)}, bf16[16,2,144,384]{3,2,1,0:T(8,128)(2,1)}) custom-call(bf16[128,576]{1,0:T(8,128)(2,1)} %get-tuple-element.130.flat_ref, bf16[128,768]{1,0:T(8,128)(2,1)} %get-tuple-element.131.da_ref, bf16[128,576]{1,0:T(8,128)(2,1)} %get-tuple-element.132.rows_ref, ...), custom_call_target="tpu_custom_call" | custom-call | flops 1000000000 | bytes 12000000 | tf_op jit(solution)/shard_map/pallas_call | solution.py:371
  265.7 3.9 collective-permute-start.58
  270.6 5.2 %collective-permute-done.52 = bf16[512,384]{1,0:T(8,128)(2,1)S(1)} collective-permute-done((bf16[512,384]{1,0:T(8,128)(2,1)S(1)}, bf16[512,384]{1,0:T(8,128)(2,1)S(1)}, u32[]{:S(2)}, u32[]{:S(2)}) %collective-permute-start.52) | collective-permute-done | bytes 393248 | tf_op jit(solution)/shard_map/ppermute | solution.py:682
  279.8 8.6 %collective-permute-done.53 = bf16[512,384]{1,0:T(8,128)(2,1)S(1)} collective-permute-done((bf16[512,384]{1,0:T(8,128)(2,1)S(1)}, bf16[512,384]{1,0:T(8,128)(2,1)S(1)}, u32[]{:S(2)}, u32[]{:S(2)}) %collective-permute-start.53) | collective-permute-done | bytes 393248 | tf_op jit(solution)/shard_map/ppermute | solution.py:682
  292.4 8.8 %collective-permute-done.54.refs_1_ = bf16[128,384]{1,0:T(8,128)(2,1)S(1)} collective-permute-done((bf16[128,384]{1,0:T(8,128)(2,1)S(1)}, bf16[128,384]{1,0:T(8,128)(2,1)S(1)}, u32[]{:S(2)}, u32[]{:S(2)}) %collective-permute-start.54) | collective-permute-done | bytes 98336 | tf_op jit(solution)/shard_map/ppermute | solution.py:682
  301.2 6.4 %collective-permute-done.55.refs_2_ = bf16[128,384]{1,0:T(8,128)(2,1)S(1)} collective-permute-done((bf16[128,384]{1,0:T(8,128)(2,1)S(1)}, bf16[128,384]{1,0:T(8,128)(2,1)S(1)}, u32[]{:S(2)}, u32[]{:S(2)}) %collective-permute-start.55) | collective-permute-done | bytes 98336 | tf_op jit(solution)/shard_map/ppermute | solution.py:682
  308.7 4.7 %collective-permute-done.56.refs_3_ = bf16[128,384]{1,0:T(8,128)(2,1)S(1)} collective-permute-done((bf16[128,384]{1,0:T(8,128)(2,1)S(1)}, bf16[128,384]{1,0:T(8,128)(2,1)S(1)}, u32[]{:S(2)}, u32[]{:S(2)}) %collective-permute-start.56) | collective-permute-done | bytes 98336 | tf_op jit(solution)/shard_map/ppermute | solution.py:682
  314.1 4.1 shard_map.208
  318.2 6.3 %shard_map.210 = (bf16[16,144,256]{2,1,0:T(8,128)(2,1)}, bf16[16,144,256]{2,1,0:T(8,128)(2,1)}) custom-call(bf16[128,576]{1,0:T(8,128)(2,1)} %get-tuple-element.143.refs_0_, bf16[128,960]{1,0:T(8,128)(2,1)} %get-tuple-element.144.refs_1_, f32[1,576]{1,0:T(1,128)} %get-tuple-element.145.refs_2_, f32[1,576]{1,0:T(1,128)} %get-tuple-element.146.refs_3_, ...), custom_call_target="tpu_custom_call" | custom-call | flops 100000000 | bytes 12000000 | tf_op jit(solution)/shard_map/pallas_call | solution.py:371
  327.0 3.4 collective-permute-start.69
  330.5 4.2 add_convert_fusion.3
  334.6 2.9 collective-permute-start.60
  340.0 13.4 %collective-permute-done.68 = bf16[2,144,384]{2,1,0:T(8,128)(2,1)S(1)} collective-permute-done((bf16[2,144,384]{2,1,0:T(8,128)(2,1)S(1)}, bf16[2,144,384]{2,1,0:T(8,128)(2,1)S(1)}, u32[]{:S(2)}, u32[]{:S(2)}) %collective-permute-start.68) | collective-permute-done | bytes 221216 | tf_op jit(solution)/shard_map/ppermute | solution.py:682
  353.4 7.5 %collective-permute-done.74 = bf16[4,144,256]{2,1,0:T(8,128)(2,1)S(1)} collective-permute-done((bf16[4,144,256]{2,1,0:T(8,128)(2,1)S(1)}, bf16[4,144,256]{2,1,0:T(8,128)(2,1)S(1)}, u32[]{:S(2)}, u32[]{:S(2)}) %collective-permute-start.74) | collective-permute-done | bytes 294944 | tf_op jit(solution)/shard_map/ppermute | solution.py:682
  364.4 3.2 collective-permute-done.72
  379.2 3.1 collective-permute-done.64
  384.5 3.9 collective-permute-start.78
  389.6 2.8 collective-permute-done.78
  392.5 2.5 collective-permute-start.83
  397.6 2.9 collective-permute-done.82
  402.3 2.7 collective-permute-start.85
  405.1 10.4 %collective-permute-start.87 = (bf16[4,144,448]{2,1,0:T(8,128)(2,1)S(1)}, bf16[4,144,448]{2,1,0:T(8,128)(2,1)S(1)}, u32[]{:S(2)}, u32[]{:S(2)}) collective-permute-start(bf16[4,144,448]{2,1,0:T(8,128)(2,1)S(1)} %pad_maximum_fusion.3.refs_0_), channel_id=1, source_target_pairs={{0,2},{2,0},{4,6},{6,4},{8,10},{10,8},{12,14},{14,12},{16,18},{18,... | collective-permute-start | bytes 1548296 | tf_op jit(solution)/shard_map/ppermute | solution.py:682
  415.5 6.2 %collective-permute-start.88 = (bf16[4,144,448]{2,1,0:T(8,128)(2,1)S(1)}, bf16[4,144,448]{2,1,0:T(8,128)(2,1)S(1)}, u32[]{:S(2)}, u32[]{:S(2)}) collective-permute-start(bf16[4,144,448]{2,1,0:T(8,128)(2,1)S(1)} %collective-permute-done.84.refs_1_), channel_id=1, source_target_pairs={{0,2},{2,0},{4,6},{6,4},{8,10},{10,8},{12,14},{14,12},{16,18},{18,... | collective-permute-start | bytes 1548296 | tf_op jit(solution)/shard_map/ppermute | solution.py:682
  421.7 7.8 %collective-permute-start.89 = (bf16[4,144,448]{2,1,0:T(8,128)(2,1)S(1)}, bf16[4,144,448]{2,1,0:T(8,128)(2,1)S(1)}, u32[]{:S(2)}, u32[]{:S(2)}) collective-permute-start(bf16[4,144,448]{2,1,0:T(8,128)(2,1)S(1)} %collective-permute-done.85.refs_2_), channel_id=1, source_target_pairs={{0,2},{2,0},{4,6},{6,4},{8,10},{10,8},{12,14},{14,12},{16,18},{18,... | collective-permute-start | bytes 1548296 | tf_op jit(solution)/shard_map/ppermute | solution.py:682
  430.5 7.4 %collective-permute-done.57 = f32[576,128]{1,0:T(8,128)S(1)} collective-permute-done((f32[576,128]{1,0:T(8,128)S(1)}, f32[576,128]{1,0:T(8,128)S(1)}, u32[]{:S(2)}, u32[]{:S(2)}) %collective-permute-start.57) | collective-permute-done | bytes 294944 | tf_op jit(solution)/shard_map/ppermute | solution.py:853
  440.8 6.0 %shard_map.211 = (f32[8,288]{1,0:T(8,128)}, f32[288,576]{1,0:T(8,128)}, f32[288,192]{1,0:T(8,128)}, f32[288,192]{1,0:T(8,128)}, f32[288,576]{1,0:T(8,128)}, /*in...) custom-call(bf16[4,144,448]{2,1,0:T(8,128)(2,1)} %copy-done.14, bf16[4,144,448]{2,1,0:T(8,128)(2,1)} %copy-done.51, ...), custom_call_target="tpu_custom_call" | custom-call | flops 100000000 | bytes 12000000 | tf_op jit(solution)/shard_map/pallas_call | solution.py:371
  (383 shorter events, 110.3 us)
Async XLA Ops:
  3.5 33.5 %collective-permute-start = (bf16[160,960]{1,0:T(8,128)(2,1)}, bf16[160,960]{1,0:T(8,128)(2,1)}, u32[]{:S(2)}, u32[]{:S(2)}) collective-permute-start(bf16[160,960]{1,0:T(8,128)(2,1)} %pad_maximum_fusion.4), channel_id=1, source_target_pairs={{0,64},{1,65},{64,0},{65,1},{2,66},{3,67},{66,2},{67,3},{4,68},{5,... | collective-permute-start | bytes 921608 | tf_op jit(solution)/shard_map/ppermute | solution.py:685
  6.0 31.0 %collective-permute-start.1 = (bf16[160,960]{1,0:T(8,128)(2,1)}, bf16[160,960]{1,0:T(8,128)(2,1)}, u32[]{:S(2)}, u32[]{:S(2)}) collective-permute-start(bf16[160,960]{1,0:T(8,128)(2,1)} %pad_maximum_fusion.4), channel_id=1, source_target_pairs={{0,1},{1,0},{64,65},{65,64},{2,3},{3,2},{66,67},{67,66},{4,5},{5,4... | collective-permute-start | bytes 921608 | tf_op jit(solution)/shard_map/ppermute | solution.py:685
  9.3 27.7 %collective-permute-start.2 = (bf16[160,960]{1,0:T(8,128)(2,1)}, bf16[160,960]{1,0:T(8,128)(2,1)}, u32[]{:S(2)}, u32[]{:S(2)}) collective-permute-start(bf16[160,960]{1,0:T(8,128)(2,1)} %pad_maximum_fusion.4), channel_id=1, source_target_pairs={{0,65},{1,64},{64,1},{65,0},{2,67},{3,66},{66,3},{67,2},{4,69},{5,... | collective-permute-start | bytes 921608 | tf_op jit(solution)/shard_map/ppermute | solution.py:685
  37.0 63.8 %collective-permute-start.16 = (bf16[144,5632]{1,0:T(8,128)(2,1)}, bf16[144,5632]{1,0:T(8,128)(2,1)S(1)}, u32[]{:S(2)}, u32[]{:S(2)}) collective-permute-start(bf16[144,5632]{1,0:T(8,128)(2,1)} %constant_dynamic-slice_fusion.1), channel_id=1, source_target_pairs={{0,64},{1,65},{64,0},{65,1},{2,66},{3,67},{66,2},{67,3},{4,68},{5,... | collective-permute-start | bytes 4866056 | tf_op jit(solution)/shard_map/ppermute | solution.py:685
  37.1 63.9 %collective-permute-start.21 = (bf16[144,5632]{1,0:T(8,128)(2,1)}, bf16[144,5632]{1,0:T(8,128)(2,1)}, u32[]{:S(2)}, u32[]{:S(2)}) collective-permute-start(bf16[144,5632]{1,0:T(8,128)(2,1)} %constant_dynamic-slice_fusion.1), channel_id=1, source_target_pairs={{0,65},{1,64},{64,1},{65,0},{2,67},{3,66},{66,3},{67,2},{4,69},{5,... | collective-permute-start | bytes 4866056 | tf_op jit(solution)/shard_map/ppermute | solution.py:685
  47.7 35.1 %collective-permute-start.17 = (bf16[144,1408]{1,0:T(8,128)(2,1)S(1)}, bf16[144,1408]{1,0:T(8,128)(2,1)S(1)}, u32[]{:S(2)}, u32[]{:S(2)}) collective-permute-start(bf16[144,1408]{1,0:T(8,128)(2,1)S(1)} %constant_dynamic-slice_fusion), channel_id=1, source_target_pairs={{0,1},{1,0},{64,65},{65,64},{2,3},{3,2},{66,67},{67,66},{4,5},{5,4... | collective-permute-start | bytes 1216520 | tf_op jit(solution)/shard_map/ppermute | solution.py:685
  55.5 27.4 %collective-permute-start.6 = (bf16[128,384]{1,0:T(8,128)(2,1)}, bf16[128,384]{1,0:T(8,128)(2,1)S(1)}, u32[]{:S(2)}, u32[]{:S(2)}) collective-permute-start(bf16[128,384]{1,0:T(8,128)(2,1)} %get-tuple-element.87), channel_id=1, source_target_pairs={{0,16},{2,6},{4,20},{6,10},{8,24},{10,14},{12,28},{14,2},{16,32},{... | collective-permute-start | bytes 294920 | tf_op jit(solution)/shard_map/ppermute | solution.py:682
  55.5 29.0 %collective-permute-start.7 = (bf16[128,384]{1,0:T(8,128)(2,1)}, bf16[128,384]{1,0:T(8,128)(2,1)S(1)}, u32[]{:S(2)}, u32[]{:S(2)}) collective-permute-start(bf16[128,384]{1,0:T(8,128)(2,1)} %get-tuple-element.87), channel_id=1, source_target_pairs={{0,32},{2,10},{4,36},{6,14},{8,40},{10,2},{12,44},{14,6},{16,48},{... | collective-permute-start | bytes 294920 | tf_op jit(solution)/shard_map/ppermute | solution.py:682
  84.5 11.2 %collective-permute-start.18 = (bf16[144,1408]{1,0:T(8,128)(2,1)S(1)}, bf16[144,1408]{1,0:T(8,128)(2,1)S(1)}, u32[]{:S(2)}, u32[]{:S(2)}) collective-permute-start(bf16[144,1408]{1,0:T(8,128)(2,1)S(1)} %collective-permute-done.17), channel_id=1, source_target_pairs={{0,16},{2,6},{4,20},{6,10},{8,24},{10,14},{12,28},{14,2},{16,32},{... | collective-permute-start | bytes 1216520 | tf_op jit(solution)/shard_map/ppermute | solution.py:682
  89.9 11.5 %collective-permute-start.8 = (bf16[128,384]{1,0:T(8,128)(2,1)}, bf16[128,384]{1,0:T(8,128)(2,1)S(1)}, u32[]{:S(2)}, u32[]{:S(2)}) collective-permute-start(bf16[128,384]{1,0:T(8,128)(2,1)} %get-tuple-element.87), channel_id=1, source_target_pairs={{0,48},{2,14},{4,52},{6,2},{8,56},{10,6},{12,60},{14,10},{16,0},{1... | collective-permute-start | bytes 294920 | tf_op jit(solution)/shard_map/ppermute | solution.py:682
  96.0 30.8 %collective-permute-start.23 = (bf16[4,144,1408]{2,1,0:T(8,128)(2,1)S(1)}, bf16[4,144,1408]{2,1,0:T(8,128)(2,1)S(1)}, u32[]{:S(2)}, u32[]{:S(2)}) collective-permute-start(bf16[4,144,1408]{2,1,0:T(8,128)(2,1)S(1)} %pad_maximum_fusion.refs_23_.refs_24_.refs_32_), channel_id=1, source_target_pairs={{0,2},{2,0},{4,6},{6,4},{8,10},{10,8},{12,14},{14,12},{16,18},{18,... | collective-permute-start | bytes 4866056 | tf_op jit(solution)/shard_map/ppermute | solution.py:682
  100.8 26.0 %collective-permute-start.22 = (bf16[144,5632]{1,0:T(8,128)(2,1)S(1)}, bf16[144,5632]{1,0:T(8,128)(2,1)S(1)}, u32[]{:S(2)}, u32[]{:S(2)}) collective-permute-start(bf16[144,5632]{1,0:T(8,128)(2,1)S(1)} %collective-permute-done.16.refs_22_.refs_23_.refs_31_), channel_id=1, source_target_pairs={{0,2},{2,0},{4,6},{6,4},{8,10},{10,8},{12,14},{14,12},{16,18},{18,... | collective-permute-start | bytes 4866056 | tf_op jit(solution)/shard_map/ppermute | solution.py:682
  100.9 25.9 %collective-permute-start.24 = (bf16[144,5632]{1,0:T(8,128)(2,1)}, bf16[144,5632]{1,0:T(8,128)(2,1)}, u32[]{:S(2)}, u32[]{:S(2)}) collective-permute-start(bf16[144,5632]{1,0:T(8,128)(2,1)} %collective-permute-done.21.refs_24_.refs_25_.refs_33_), channel_id=1, source_target_pairs={{0,2},{2,0},{4,6},{6,4},{8,10},{10,8},{12,14},{14,12},{16,18},{18,... | collective-permute-start | bytes 4866056 | tf_op jit(solution)/shard_map/ppermute | solution.py:682
  101.4 12.4 %collective-permute-start.9 = (bf16[512,384]{1,0:T(8,128)(2,1)S(1)}, bf16[512,384]{1,0:T(8,128)(2,1)S(1)}, u32[]{:S(2)}, u32[]{:S(2)}) collective-permute-start(bf16[512,384]{1,0:T(8,128)(2,1)S(1)} %constant_dynamic-update-slice_fusion.refs_0_), channel_id=1, source_target_pairs={{0,4},{2,18},{4,8},{6,22},{8,12},{10,26},{12,0},{14,30},{16,20},{1... | collective-permute-start | bytes 1179656 | tf_op jit(solution)/shard_map/ppermute | solution.py:682
  101.7 12.1 %collective-permute-start.10 = (bf16[512,384]{1,0:T(8,128)(2,1)S(1)}, bf16[512,384]{1,0:T(8,128)(2,1)S(1)}, u32[]{:S(2)}, u32[]{:S(2)}) collective-permute-start(bf16[512,384]{1,0:T(8,128)(2,1)S(1)} %constant_dynamic-update-slice_fusion.refs_0_), channel_id=1, source_target_pairs={{0,8},{2,34},{4,12},{6,38},{8,0},{10,42},{12,4},{14,46},{16,24},{1... | collective-permute-start | bytes 1179656 | tf_op jit(solution)/shard_map/ppermute | solution.py:682
  151.1 12.4 %collective-permute-start.28 = (bf16[512,384]{1,0:T(8,128)(2,1)S(1)}, bf16[512,384]{1,0:T(8,128)(2,1)S(1)}, u32[]{:S(2)}, u32[]{:S(2)}) collective-permute-start(bf16[512,384]{1,0:T(8,128)(2,1)S(1)} %constant_dynamic-update-slice_fusion.4.refs_0_), channel_id=1, source_target_pairs={{0,4},{2,18},{4,8},{6,22},{8,12},{10,26},{12,0},{14,30},{16,20},{1... | collective-permute-start | bytes 1179656 | tf_op jit(solution)/shard_map/ppermute | solution.py:682
  151.2 14.6 %collective-permute-start.29 = (bf16[512,384]{1,0:T(8,128)(2,1)S(1)}, bf16[512,384]{1,0:T(8,128)(2,1)S(1)}, u32[]{:S(2)}, u32[]{:S(2)}) collective-permute-start(bf16[512,384]{1,0:T(8,128)(2,1)S(1)} %constant_dynamic-update-slice_fusion.4.refs_0_), channel_id=1, source_target_pairs={{0,8},{2,34},{4,12},{6,38},{8,0},{10,42},{12,4},{14,46},{16,24},{1... | collective-permute-start | bytes 1179656 | tf_op jit(solution)/shard_map/ppermute | solution.py:682
  152.9 13.0 %collective-permute-start.30 = (bf16[512,384]{1,0:T(8,128)(2,1)S(1)}, bf16[512,384]{1,0:T(8,128)(2,1)S(1)}, u32[]{:S(2)}, u32[]{:S(2)}) collective-permute-start(bf16[512,384]{1,0:T(8,128)(2,1)S(1)} %constant_dynamic-update-slice_fusion.4.refs_0_), channel_id=1, source_target_pairs={{0,12},{2,50},{4,0},{6,54},{8,4},{10,58},{12,8},{14,62},{16,28},{1... | collective-permute-start | bytes 1179656 | tf_op jit(solution)/shard_map/ppermute | solution.py:682
  154.9 12.5 %collective-permute-start.31 = (bf16[512,384]{1,0:T(8,128)(2,1)S(1)}, bf16[512,384]{1,0:T(8,128)(2,1)S(1)}, u32[]{:S(2)}, u32[]{:S(2)}) collective-permute-start(bf16[512,384]{1,0:T(8,128)(2,1)S(1)} %constant_dynamic-update-slice_fusion.4.refs_0_), channel_id=1, source_target_pairs={{0,2},{2,0},{4,6},{6,4},{8,10},{10,8},{12,14},{14,12},{16,18},{18,... | collective-permute-start | bytes 1179656 | tf_op jit(solution)/shard_map/ppermute | solution.py:682
  206.7 23.5 %collective-permute-start.46 = (bf16[16,2,144,384]{3,2,1,0:T(8,128)(2,1)}, bf16[16,2,144,384]{3,2,1,0:T(8,128)(2,1)S(1)}, u32[]{:S(2)}, u32[]{:S(2)}) collective-permute-start(bf16[16,2,144,384]{3,2,1,0:T(8,128)(2,1)} %get-tuple-element.113), channel_id=1, source_target_pairs={{0,2},{2,0},{4,6},{6,4},{8,10},{10,8},{12,14},{14,12},{16,18},{18,... | collective-permute-start | bytes 10616840 | tf_op jit(solution)/shard_map/ppermute | solution.py:682
  207.7 10.0 %collective-permute-start.37 = (bf16[512,384]{1,0:T(8,128)(2,1)S(1)}, bf16[512,384]{1,0:T(8,128)(2,1)S(1)}, u32[]{:S(2)}, u32[]{:S(2)}) collective-permute-start(bf16[512,384]{1,0:T(8,128)(2,1)S(1)} %copy-done.62), channel_id=1, source_target_pairs={{0,2},{2,0},{4,6},{6,4},{8,10},{10,8},{12,14},{14,12},{16,18},{18,... | collective-permute-start | bytes 1179656 | tf_op jit(solution)/shard_map/ppermute | solution.py:682
  207.8 10.1 %collective-permute-start.36 = (bf16[512,384]{1,0:T(8,128)(2,1)S(1)}, bf16[512,384]{1,0:T(8,128)(2,1)S(1)}, u32[]{:S(2)}, u32[]{:S(2)}) collective-permute-start(bf16[512,384]{1,0:T(8,128)(2,1)S(1)} %copy-done.60), channel_id=1, source_target_pairs={{0,2},{2,0},{4,6},{6,4},{8,10},{10,8},{12,14},{14,12},{16,18},{18,... | collective-permute-start | bytes 1179656 | tf_op jit(solution)/shard_map/ppermute | solution.py:682
  214.9 11.9 %collective-permute-start.40 = (bf16[512,384]{1,0:T(8,128)(2,1)S(1)}, bf16[512,384]{1,0:T(8,128)(2,1)S(1)}, u32[]{:S(2)}, u32[]{:S(2)}) collective-permute-start(bf16[512,384]{1,0:T(8,128)(2,1)S(1)} %add_convert_fusion.15), channel_id=1, source_target_pairs={{0,8},{2,34},{4,12},{6,38},{8,0},{10,42},{12,4},{14,46},{16,24},{1... | collective-permute-start | bytes 1179656 | tf_op jit(solution)/shard_map/ppermute | solution.py:682
  217.8 9.3 %collective-permute-start.38 = (bf16[512,384]{1,0:T(8,128)(2,1)S(1)}, bf16[512,384]{1,0:T(8,128)(2,1)S(1)}, u32[]{:S(2)}, u32[]{:S(2)}) collective-permute-start(bf16[512,384]{1,0:T(8,128)(2,1)S(1)} %add_convert_fusion.16), channel_id=1, source_target_pairs={{0,12},{2,50},{4,0},{6,54},{8,4},{10,58},{12,8},{14,62},{16,28},{1... | collective-permute-start | bytes 1179656 | tf_op jit(solution)/shard_map/ppermute | solution.py:682
  265.7 64.8 %collective-permute-start.58 = (bf16[16,2,144,384]{3,2,1,0:T(8,128)(2,1)}, bf16[16,2,144,384]{3,2,1,0:T(8,128)(2,1)}, u32[]{:S(2)}, u32[]{:S(2)}) collective-permute-start(bf16[16,2,144,384]{3,2,1,0:T(8,128)(2,1)} %get-tuple-element.138), channel_id=1, source_target_pairs={{0,2},{2,0},{4,6},{6,4},{8,10},{10,8},{12,14},{14,12},{16,18},{18,... | collective-permute-start | bytes 10616840 | tf_op jit(solution)/shard_map/ppermute | solution.py:682
  276.0 12.4 %collective-permute-start.53 = (bf16[512,384]{1,0:T(8,128)(2,1)S(1)}, bf16[512,384]{1,0:T(8,128)(2,1)S(1)}, u32[]{:S(2)}, u32[]{:S(2)}) collective-permute-start(bf16[512,384]{1,0:T(8,128)(2,1)S(1)} %add_convert_fusion.9), channel_id=1, source_target_pairs={{0,4},{2,18},{4,8},{6,22},{8,12},{10,26},{12,0},{14,30},{16,20},{1... | collective-permute-start | bytes 1179656 | tf_op jit(solution)/shard_map/ppermute | solution.py:682
  276.5 11.9 %collective-permute-start.51 = (bf16[512,384]{1,0:T(8,128)(2,1)S(1)}, bf16[512,384]{1,0:T(8,128)(2,1)S(1)}, u32[]{:S(2)}, u32[]{:S(2)}) collective-permute-start(bf16[512,384]{1,0:T(8,128)(2,1)S(1)} %add_convert_fusion.10), channel_id=1, source_target_pairs={{0,8},{2,34},{4,12},{6,38},{8,0},{10,42},{12,4},{14,46},{16,24},{1... | collective-permute-start | bytes 1179656 | tf_op jit(solution)/shard_map/ppermute | solution.py:682
  277.8 11.4 %collective-permute-start.49 = (bf16[512,384]{1,0:T(8,128)(2,1)S(1)}, bf16[512,384]{1,0:T(8,128)(2,1)S(1)}, u32[]{:S(2)}, u32[]{:S(2)}) collective-permute-start(bf16[512,384]{1,0:T(8,128)(2,1)S(1)} %add_convert_fusion.11), channel_id=1, source_target_pairs={{0,12},{2,50},{4,0},{6,54},{8,4},{10,58},{12,8},{14,62},{16,28},{1... | collective-permute-start | bytes 1179656 | tf_op jit(solution)/shard_map/ppermute | solution.py:682
  279.3 46.4 %collective-permute-start.67 = (bf16[4,2,144,384]{3,2,1,0:T(8,128)(2,1)}, bf16[4,2,144,384]{3,2,1,0:T(8,128)(2,1)S(1)}, u32[]{:S(2)}, u32[]{:S(2)}) collective-permute-start(bf16[4,2,144,384]{3,2,1,0:T(8,128)(2,1)} %get-tuple-element.142), channel_id=1, source_target_pairs={{0,4},{2,18},{4,8},{6,22},{8,12},{10,26},{12,0},{14,30},{16,20},{1... | collective-permute-start | bytes 2654216 | tf_op jit(solution)/shard_map/ppermute | solution.py:682
  288.4 37.4 %collective-permute-start.66 = (bf16[4,2,144,384]{3,2,1,0:T(8,128)(2,1)}, bf16[4,2,144,384]{3,2,1,0:T(8,128)(2,1)S(1)}, u32[]{:S(2)}, u32[]{:S(2)}) collective-permute-start(bf16[4,2,144,384]{3,2,1,0:T(8,128)(2,1)} %get-tuple-element.141), channel_id=1, source_target_pairs={{0,8},{2,34},{4,12},{6,38},{8,0},{10,42},{12,4},{14,46},{16,24},{1... | collective-permute-start | bytes 2654216 | tf_op jit(solution)/shard_map/ppermute | solution.py:682
  288.4 37.4 %collective-permute-start.65 = (bf16[4,2,144,384]{3,2,1,0:T(8,128)(2,1)}, bf16[4,2,144,384]{3,2,1,0:T(8,128)(2,1)S(1)}, u32[]{:S(2)}, u32[]{:S(2)}) collective-permute-start(bf16[4,2,144,384]{3,2,1,0:T(8,128)(2,1)} %get-tuple-element.140), channel_id=1, source_target_pairs={{0,12},{2,50},{4,0},{6,54},{8,4},{10,58},{12,8},{14,62},{16,28},{1... | collective-permute-start | bytes 2654216 | tf_op jit(solution)/shard_map/ppermute | solution.py:682
  290.1 11.1 %collective-permute-start.54 = (bf16[128,384]{1,0:T(8,128)(2,1)S(1)}, bf16[128,384]{1,0:T(8,128)(2,1)S(1)}, u32[]{:S(2)}, u32[]{:S(2)}) collective-permute-start(bf16[128,384]{1,0:T(8,128)(2,1)S(1)} %get-tuple-element.226), channel_id=1, source_target_pairs={{0,48},{2,14},{4,52},{6,2},{8,56},{10,6},{12,60},{14,10},{16,0},{1... | collective-permute-start | bytes 294920 | tf_op jit(solution)/shard_map/ppermute | solution.py:682
  324.5 13.0 %collective-permute-start.71 = (bf16[16,144,256]{2,1,0:T(8,128)(2,1)}, bf16[16,144,256]{2,1,0:T(8,128)(2,1)S(1)}, u32[]{:S(2)}, u32[]{:S(2)}) collective-permute-start(bf16[16,144,256]{2,1,0:T(8,128)(2,1)} %get-tuple-element.152), channel_id=1, source_target_pairs={{0,2},{2,0},{4,6},{6,4},{8,10},{10,8},{12,14},{14,12},{16,18},{18,... | collective-permute-start | bytes 3538952 | tf_op jit(solution)/shard_map/ppermute | solution.py:682
  327.0 11.6 %collective-permute-start.70 = (bf16[2,144,384]{2,1,0:T(8,128)(2,1)S(1)}, bf16[2,144,384]{2,1,0:T(8,128)(2,1)S(1)}, u32[]{:S(2)}, u32[]{:S(2)}) collective-permute-start(bf16[2,144,384]{2,1,0:T(8,128)(2,1)S(1)} %get-tuple-element.208), channel_id=1, source_target_pairs={{0,16},{2,6},{4,20},{6,10},{8,24},{10,14},{12,28},{14,2},{16,32},{... | collective-permute-start | bytes 663560 | tf_op jit(solution)/shard_map/ppermute | solution.py:682
  327.0 13.0 %collective-permute-start.69 = (bf16[2,144,384]{2,1,0:T(8,128)(2,1)S(1)}, bf16[2,144,384]{2,1,0:T(8,128)(2,1)S(1)}, u32[]{:S(2)}, u32[]{:S(2)}) collective-permute-start(bf16[2,144,384]{2,1,0:T(8,128)(2,1)S(1)} %get-tuple-element.209), channel_id=1, source_target_pairs={{0,32},{2,10},{4,36},{6,14},{8,40},{10,2},{12,44},{14,6},{16,48},{... | collective-permute-start | bytes 663560 | tf_op jit(solution)/shard_map/ppermute | solution.py:682
  334.6 35.2 %collective-permute-start.61 = (bf16[4,2,144,384]{3,2,1,0:T(8,128)(2,1)}, bf16[4,2,144,384]{3,2,1,0:T(8,128)(2,1)}, u32[]{:S(2)}, u32[]{:S(2)}) collective-permute-start(bf16[4,2,144,384]{3,2,1,0:T(8,128)(2,1)} %get-tuple-element.197), channel_id=1, source_target_pairs={{0,4},{2,18},{4,8},{6,22},{8,12},{10,26},{12,0},{14,30},{16,20},{1... | collective-permute-start | bytes 2654216 | tf_op jit(solution)/shard_map/ppermute | solution.py:682
  334.6 37.0 %collective-permute-start.60 = (bf16[4,2,144,384]{3,2,1,0:T(8,128)(2,1)}, bf16[4,2,144,384]{3,2,1,0:T(8,128)(2,1)}, u32[]{:S(2)}, u32[]{:S(2)}) collective-permute-start(bf16[4,2,144,384]{3,2,1,0:T(8,128)(2,1)} %get-tuple-element.198), channel_id=1, source_target_pairs={{0,8},{2,34},{4,12},{6,38},{8,0},{10,42},{12,4},{14,46},{16,24},{1... | collective-permute-start | bytes 2654216 | tf_op jit(solution)/shard_map/ppermute | solution.py:682
  337.6 34.0 %collective-permute-start.59 = (bf16[4,2,144,384]{3,2,1,0:T(8,128)(2,1)}, bf16[4,2,144,384]{3,2,1,0:T(8,128)(2,1)}, u32[]{:S(2)}, u32[]{:S(2)}) collective-permute-start(bf16[4,2,144,384]{3,2,1,0:T(8,128)(2,1)} %get-tuple-element.199), channel_id=1, source_target_pairs={{0,12},{2,50},{4,0},{6,54},{8,4},{10,58},{12,8},{14,62},{16,28},{1... | collective-permute-start | bytes 2654216 | tf_op jit(solution)/shard_map/ppermute | solution.py:682
  338.6 22.3 %collective-permute-start.74 = (bf16[4,144,256]{2,1,0:T(8,128)(2,1)S(1)}, bf16[4,144,256]{2,1,0:T(8,128)(2,1)S(1)}, u32[]{:S(2)}, u32[]{:S(2)}) collective-permute-start(bf16[4,144,256]{2,1,0:T(8,128)(2,1)S(1)} %get-tuple-element.211), channel_id=1, source_target_pairs={{0,4},{2,18},{4,8},{6,22},{8,12},{10,26},{12,0},{14,30},{16,20},{1... | collective-permute-start | bytes 884744 | tf_op jit(solution)/shard_map/ppermute | solution.py:682
  340.0 13.4 %collective-permute-start.68 = (bf16[2,144,384]{2,1,0:T(8,128)(2,1)S(1)}, bf16[2,144,384]{2,1,0:T(8,128)(2,1)S(1)}, u32[]{:S(2)}, u32[]{:S(2)}) collective-permute-start(bf16[2,144,384]{2,1,0:T(8,128)(2,1)S(1)} %get-tuple-element.207), channel_id=1, source_target_pairs={{0,48},{2,14},{4,52},{6,2},{8,56},{10,6},{12,60},{14,10},{16,0},{1... | collective-permute-start | bytes 663560 | tf_op jit(solution)/shard_map/ppermute | solution.py:682
  353.4 11.0 %collective-permute-start.73 = (bf16[4,144,256]{2,1,0:T(8,128)(2,1)}, bf16[4,144,256]{2,1,0:T(8,128)(2,1)}, u32[]{:S(2)}, u32[]{:S(2)}) collective-permute-start(bf16[4,144,256]{2,1,0:T(8,128)(2,1)} %get-tuple-element.212), channel_id=1, source_target_pairs={{0,8},{2,34},{4,12},{6,38},{8,0},{10,42},{12,4},{14,46},{16,24},{1... | collective-permute-start | bytes 884744 | tf_op jit(solution)/shard_map/ppermute | solution.py:682
  402.2 13.3 %collective-permute-start.84 = (bf16[4,144,448]{2,1,0:T(8,128)(2,1)S(1)}, bf16[4,144,448]{2,1,0:T(8,128)(2,1)S(1)}, u32[]{:S(2)}, u32[]{:S(2)}) collective-permute-start(bf16[4,144,448]{2,1,0:T(8,128)(2,1)S(1)} %pad_maximum_fusion.3.refs_0_), channel_id=1, source_target_pairs={{0,4},{2,18},{4,8},{6,22},{8,12},{10,26},{12,0},{14,30},{16,20},{1... | collective-permute-start | bytes 1548296 | tf_op jit(solution)/shard_map/ppermute | solution.py:682
  402.3 19.4 %collective-permute-start.85 = (bf16[4,144,448]{2,1,0:T(8,128)(2,1)S(1)}, bf16[4,144,448]{2,1,0:T(8,128)(2,1)S(1)}, u32[]{:S(2)}, u32[]{:S(2)}) collective-permute-start(bf16[4,144,448]{2,1,0:T(8,128)(2,1)S(1)} %pad_maximum_fusion.3.refs_0_), channel_id=1, source_target_pairs={{0,8},{2,34},{4,12},{6,38},{8,0},{10,42},{12,4},{14,46},{16,24},{1... | collective-permute-start | bytes 1548296 | tf_op jit(solution)/shard_map/ppermute | solution.py:682
  405.0 24.5 %collective-permute-start.86 = (bf16[4,144,448]{2,1,0:T(8,128)(2,1)S(1)}, bf16[4,144,448]{2,1,0:T(8,128)(2,1)}, u32[]{:S(2)}, u32[]{:S(2)}) collective-permute-start(bf16[4,144,448]{2,1,0:T(8,128)(2,1)S(1)} %pad_maximum_fusion.3.refs_0_), channel_id=1, source_target_pairs={{0,12},{2,50},{4,0},{6,54},{8,4},{10,58},{12,8},{14,62},{16,28},{1... | collective-permute-start | bytes 1548296 | tf_op jit(solution)/shard_map/ppermute | solution.py:682
  405.0 24.6 %collective-permute-start.35 = (bf16[576,128]{1,0:T(8,128)(2,1)S(1)}, bf16[576,128]{1,0:T(8,128)(2,1)S(1)}, u32[]{:S(2)}, u32[]{:S(2)}) collective-permute-start(bf16[576,128]{1,0:T(8,128)(2,1)S(1)} %get-tuple-element.233), channel_id=1, source_target_pairs={{0,64},{64,0},{1,65},{65,1},{2,66},{66,2},{3,67},{67,3},{4,68},{68... | collective-permute-start | bytes 442376 | tf_op jit(solution)/shard_map/ppermute | solution.py:853
  405.1 33.6 %collective-permute-start.87 = (bf16[4,144,448]{2,1,0:T(8,128)(2,1)S(1)}, bf16[4,144,448]{2,1,0:T(8,128)(2,1)S(1)}, u32[]{:S(2)}, u32[]{:S(2)}) collective-permute-start(bf16[4,144,448]{2,1,0:T(8,128)(2,1)S(1)} %pad_maximum_fusion.3.refs_0_), channel_id=1, source_target_pairs={{0,2},{2,0},{4,6},{6,4},{8,10},{10,8},{12,14},{14,12},{16,18},{18,... | collective-permute-start | bytes 1548296 | tf_op jit(solution)/shard_map/ppermute | solution.py:682
  415.5 23.2 %collective-permute-start.88 = (bf16[4,144,448]{2,1,0:T(8,128)(2,1)S(1)}, bf16[4,144,448]{2,1,0:T(8,128)(2,1)S(1)}, u32[]{:S(2)}, u32[]{:S(2)}) collective-permute-start(bf16[4,144,448]{2,1,0:T(8,128)(2,1)S(1)} %collective-permute-done.84.refs_1_), channel_id=1, source_target_pairs={{0,2},{2,0},{4,6},{6,4},{8,10},{10,8},{12,14},{14,12},{16,18},{18,... | collective-permute-start | bytes 1548296 | tf_op jit(solution)/shard_map/ppermute | solution.py:682
  421.7 17.0 %collective-permute-start.89 = (bf16[4,144,448]{2,1,0:T(8,128)(2,1)S(1)}, bf16[4,144,448]{2,1,0:T(8,128)(2,1)S(1)}, u32[]{:S(2)}, u32[]{:S(2)}) collective-permute-start(bf16[4,144,448]{2,1,0:T(8,128)(2,1)S(1)} %collective-permute-done.85.refs_2_), channel_id=1, source_target_pairs={{0,2},{2,0},{4,6},{6,4},{8,10},{10,8},{12,14},{14,12},{16,18},{18,... | collective-permute-start | bytes 1548296 | tf_op jit(solution)/shard_map/ppermute | solution.py:682
  (122 other events, 1096.5 us)
